TPU v7x, 128 devices: a whole 4x4x4 slice. The times are simulated.
128 devices in a mesh: section: 8 (over z, core), kfac: 16 (over y, x).
Axes of the slice: x: 4, y: 4, z: 4, core: 2. Of those that a mesh axis runs over, the one named last changes fastest.
Arguments:
- top_cotangent: bfloat16 [8, 32, 8192], P(None, None, 'kfac'), may hold values from -6 to 6
- inputs: bfloat16 [8, 8, 32, 8192], P('section'), may hold values from -6 to 6
- proj_weight: bfloat16 [8, 8192, 2048], P('section', None, 'kfac'), may hold values from -0.0625 to 0.0625
- return_weight: bfloat16 [8, 2048, 8192], P('section', 'kfac'), may hold values from -0.125 to 0.125
- owners: int32 [8, 8], P('section'), may hold values from 0 to 15, as said below
- input_inverses: bfloat16 [8, 16, 1024, 1024], P('section', 'kfac'), as said below
- output_inverses: bfloat16 [8, 2, 1024, 1024], P('section'), as said below
Outputs:
- section_cotangents: bfloat16 [8, 8, 32, 8192], P('section', None, None, 'kfac')
- preconditioned: bfloat16 [8, 8192, 2048], P('section', None, 'kfac')
Inputs may be any that keep to these rules, and one draw needn't show every extreme that they name: In each section's row no kfac device is named more than once (the eight blocks of a section have eight distinct owners). `input_inverses`: slot o + j of a section holds the inverse for the (j+1)-th block, in block order, that owners assigns to device o; slots that no block uses hold arbitrary values. Each block is symmetric. `output_inverses`: each block is symmetric.
All inputs are finite; a program needn't handle non-finite values.
Results may differ from a plain program's by a relative error of at most 0.035.
Values may be sent and summed in bfloat16 or wider, within the bound.
No kernel may reach another device: no remote copies, remote signals or barrier semaphores. Data moves between devices by JAX's collectives and lax.ppermute only.
A program may use at most 128 MiB of HBM per device.

v0:
```python
import jax
import jax.numpy as jnp
from jax import lax
from jax.sharding import PartitionSpec as P


def from_behind(block, axis, distance):
    devices = range(lax.axis_size(axis))
    route = [(i - distance, i) for i in devices if i - distance in devices]
    return lax.ppermute(block, axis, route)


def silu_slope(values):
    sigmoid = jax.nn.sigmoid(values)
    return sigmoid * (1.0 + values * (1.0 - sigmoid))


def slot_numbers(owner_row):
    blocks = owner_row.shape[0]
    earlier = jnp.arange(blocks)[None, :] < jnp.arange(blocks)[:, None]
    shared = owner_row[None, :] == owner_row[:, None]
    return jnp.sum(jnp.logical_and(earlier, shared).astype(jnp.int32), axis=1)


def on_device(
    top_cotangent, inputs, proj_weight, return_weight, owners, input_inverses, output_inverses
):
    section_count = lax.axis_size("section")
    section_here = lax.axis_index("section")
    kfac_count = lax.axis_size("kfac")
    micro_count, token_count, shard_width = top_cotangent.shape
    activations = inputs[0]
    weight = proj_weight[0]
    returning = return_weight[0]
    model_width, stripe_width = weight.shape
    slot_count = input_inverses.shape[1]
    block_width = input_inverses.shape[2]
    block_count = model_width // block_width
    group_count = output_inverses.shape[1]

    def one_tick(tick_now, loop_state):
        incoming, outputs, slope_all = loop_state
        micro_now = tick_now - (section_count - 1 - section_here)
        valid = jnp.logical_and(micro_now >= 0, micro_now < micro_count)
        micro_safe = jnp.clip(micro_now, 0, micro_count - 1)
        from_top = lax.dynamic_index_in_dim(top_cotangent, micro_safe, 0, keepdims=False)
        shard = jnp.where(section_here == section_count - 1, from_top, incoming)
        whole = lax.all_gather(shard, "kfac", axis=1, tiled=True)
        tokens_now = lax.dynamic_index_in_dim(activations, micro_safe, 0, keepdims=False)
        hidden = jnp.dot(tokens_now, weight, preferred_element_type=jnp.float32)
        returned = jnp.einsum("td,cd->tc", whole, returning, preferred_element_type=jnp.float32)
        slope_grad = (returned * silu_slope(hidden)).astype(jnp.bfloat16)
        partial_terms = jnp.einsum(
            "tc,dc->td", slope_grad, weight, preferred_element_type=jnp.float32
        )
        summed = lax.psum_scatter(
            partial_terms.astype(jnp.bfloat16), "kfac", scatter_dimension=1, tiled=True
        ).astype(jnp.float32)
        updated = (shard.astype(jnp.float32) + summed).astype(jnp.bfloat16)
        outputs = jnp.where(
            valid, lax.dynamic_update_index_in_dim(outputs, updated, micro_safe, 0), outputs
        )
        slope_all = jnp.where(
            valid, lax.dynamic_update_index_in_dim(slope_all, slope_grad, micro_safe, 0), slope_all
        )
        passed = from_behind(updated, "section", -1)
        return (passed, outputs, slope_all)

    start_state = (
        jnp.zeros((token_count, shard_width), jnp.bfloat16),
        jnp.zeros((micro_count, token_count, shard_width), jnp.bfloat16),
        jnp.zeros((micro_count, token_count, stripe_width), jnp.bfloat16),
    )
    final_state = lax.fori_loop(0, section_count + micro_count - 1, one_tick, start_state)
    outputs = final_state[1]
    slope_all = final_state[2]
    owner_row = owners[0]
    slot_ids = slot_numbers(owner_row)
    target = owner_row * slot_count + slot_ids
    positions = jnp.arange(kfac_count * slot_count, dtype=jnp.int32)
    selector_int = (positions[:, None] == target[None, :]).astype(jnp.int32)
    selector = selector_int.astype(jnp.bfloat16)
    flat_tokens = activations.reshape(micro_count * token_count, model_width)
    flat_slopes = slope_all.reshape(micro_count * token_count, stripe_width)
    gradient = jnp.einsum(
        "rd,rc->dc", flat_tokens, flat_slopes, preferred_element_type=jnp.float32
    ).astype(jnp.bfloat16)
    pieces = gradient.reshape(block_count, block_width, stripe_width)
    outgoing = jnp.einsum(
        "sb,bic->sic", selector, pieces, preferred_element_type=jnp.float32
    ).astype(jnp.bfloat16)
    outgoing = outgoing.reshape(kfac_count, slot_count, block_width, stripe_width)
    arrived = lax.all_to_all(outgoing, "kfac", split_axis=0, concat_axis=3, tiled=True)
    gathered_grad = arrived.reshape(slot_count, block_width, kfac_count * stripe_width)
    left_product = jnp.einsum(
        "sij,sjc->sic", input_inverses[0], gathered_grad, preferred_element_type=jnp.float32
    ).astype(jnp.bfloat16)
    split_groups = left_product.reshape(slot_count, block_width, group_count, block_width)
    right_product = jnp.einsum(
        "sinj,njk->sink", split_groups, output_inverses[0], preferred_element_type=jnp.float32
    ).astype(jnp.bfloat16)
    sendback = right_product.reshape(1, slot_count, block_width, group_count * block_width)
    returned_blocks = lax.all_to_all(sendback, "kfac", split_axis=3, concat_axis=0, tiled=True)
    flat_returned = returned_blocks.reshape(kfac_count * slot_count, block_width, stripe_width)
    stripe = jnp.einsum(
        "sb,sic->bic", selector, flat_returned, preferred_element_type=jnp.float32
    ).astype(jnp.bfloat16)
    stripe = stripe.reshape(model_width, stripe_width)
    return (outputs[None], stripe[None])


def solution(mesh):
    return jax.shard_map(
        on_device,
        mesh=mesh,
        in_specs=(
            P(None, None, "kfac"),
            P("section", None, None, None),
            P("section", None, "kfac"),
            P("section", "kfac", None),
            P("section", None),
            P("section", "kfac", None, None),
            P("section", None, None, None),
        ),
        out_specs=(P("section", None, None, "kfac"), P("section", None, "kfac")),
        check_vma=False,
    )
```

profile of v0, /device:TPU:0, one launch (start us, length us, event | category | flops | bytes accessed | tf_op | source)
XLA Modules:
  0.0 1857.2 jit_solution(8969292306528276908)
XLA Ops:
  8.9 1593.8 %while.19 = (s32[]{:T(128)}, bf16[32,512]{1,0:T(8,128)(2,1)S(1)}, bf16[8,32,512]{2,1,0:T(8,128)(2,1)S(1)}, bf16[8,32,128]{2,1,0:T(8,128)(2,1)S(1)}, pred[]{:T(51...) while((s32[]{:T(128)}, bf16[32,512]{1,0:T(8,128)(2,1)S(1)}, ...), condition=%wide.region_2.3_spmd, body=%wide.region_0.2_spmd.sunk | while | flops 201728000 | bytes 18940220 | solution.py:74
  9.7 24.3 %all_gather.10 = bf16[32,8192]{1,0:T(8,128)(2,1)S(1)} all-gather(bf16[32,512]{1,0:T(8,128)(2,1)S(1)} %bitcast_select_fusion.4), channel_id=1, replica_groups=mesh['section'=8,'kfac'=16] {'kfac'}, dimensions={1}, use_global_device_ids=true | all-gather | bytes 557056 | tf_op jit(solution)/shard_map/while/body/eval_jaxpr/all_gather | solution.py:48
  40.5 72.6 %reduce-scatter.2.cloned.1.call-done = bf16[32,512]{1,0:T(8,128)(2,1)} async-done(((bf16[32,8192]{1,0:T(8,128)(2,1)}), bf16[32,512]{1,0:T(8,128)(2,1)}) %reduce-scatter.2.cloned.1.call-update) | async-done | bytes 32784 | tf_op jit(solution)/shard_map/while/body/eval_jaxpr/reduce_scatter | solution.py:56
  147.5 71.7 %reduce-scatter.2.cloned.1.call-done = bf16[32,512]{1,0:T(8,128)(2,1)} async-done(((bf16[32,8192]{1,0:T(8,128)(2,1)}), bf16[32,512]{1,0:T(8,128)(2,1)}) %reduce-scatter.2.cloned.1.call-update) | async-done | bytes 32784 | tf_op jit(solution)/shard_map/while/body/eval_jaxpr/reduce_scatter | solution.py:56
  253.6 71.7 %reduce-scatter.2.cloned.1.call-done = bf16[32,512]{1,0:T(8,128)(2,1)} async-done(((bf16[32,8192]{1,0:T(8,128)(2,1)}), bf16[32,512]{1,0:T(8,128)(2,1)}) %reduce-scatter.2.cloned.1.call-update) | async-done | bytes 32784 | tf_op jit(solution)/shard_map/while/body/eval_jaxpr/reduce_scatter | solution.py:56
  359.7 71.7 %reduce-scatter.2.cloned.1.call-done = bf16[32,512]{1,0:T(8,128)(2,1)} async-done(((bf16[32,8192]{1,0:T(8,128)(2,1)}), bf16[32,512]{1,0:T(8,128)(2,1)}) %reduce-scatter.2.cloned.1.call-update) | async-done | bytes 32784 | tf_op jit(solution)/shard_map/while/body/eval_jaxpr/reduce_scatter | solution.py:56
  436.1 23.3 %all_gather.10 = bf16[32,8192]{1,0:T(8,128)(2,1)S(1)} all-gather(bf16[32,512]{1,0:T(8,128)(2,1)S(1)} %bitcast_select_fusion.4), channel_id=1, replica_groups=mesh['section'=8,'kfac'=16] {'kfac'}, dimensions={1}, use_global_device_ids=true | all-gather | bytes 557056 | tf_op jit(solution)/shard_map/while/body/eval_jaxpr/all_gather | solution.py:48
  465.8 71.7 %reduce-scatter.2.cloned.1.call-done = bf16[32,512]{1,0:T(8,128)(2,1)} async-done(((bf16[32,8192]{1,0:T(8,128)(2,1)}), bf16[32,512]{1,0:T(8,128)(2,1)}) %reduce-scatter.2.cloned.1.call-update) | async-done | bytes 32784 | tf_op jit(solution)/shard_map/while/body/eval_jaxpr/reduce_scatter | solution.py:56
  571.9 71.7 %reduce-scatter.2.cloned.1.call-done = bf16[32,512]{1,0:T(8,128)(2,1)} async-done(((bf16[32,8192]{1,0:T(8,128)(2,1)}), bf16[32,512]{1,0:T(8,128)(2,1)}) %reduce-scatter.2.cloned.1.call-update) | async-done | bytes 32784 | tf_op jit(solution)/shard_map/while/body/eval_jaxpr/reduce_scatter | solution.py:56
  648.3 23.4 %all_gather.10 = bf16[32,8192]{1,0:T(8,128)(2,1)S(1)} all-gather(bf16[32,512]{1,0:T(8,128)(2,1)S(1)} %bitcast_select_fusion.4), channel_id=1, replica_groups=mesh['section'=8,'kfac'=16] {'kfac'}, dimensions={1}, use_global_device_ids=true | all-gather | bytes 557056 | tf_op jit(solution)/shard_map/while/body/eval_jaxpr/all_gather | solution.py:48
  678.1 71.7 %reduce-scatter.2.cloned.1.call-done = bf16[32,512]{1,0:T(8,128)(2,1)} async-done(((bf16[32,8192]{1,0:T(8,128)(2,1)}), bf16[32,512]{1,0:T(8,128)(2,1)}) %reduce-scatter.2.cloned.1.call-update) | async-done | bytes 32784 | tf_op jit(solution)/shard_map/while/body/eval_jaxpr/reduce_scatter | solution.py:56
  754.4 23.3 %all_gather.10 = bf16[32,8192]{1,0:T(8,128)(2,1)S(1)} all-gather(bf16[32,512]{1,0:T(8,128)(2,1)S(1)} %bitcast_select_fusion.4), channel_id=1, replica_groups=mesh['section'=8,'kfac'=16] {'kfac'}, dimensions={1}, use_global_device_ids=true | all-gather | bytes 557056 | tf_op jit(solution)/shard_map/while/body/eval_jaxpr/all_gather | solution.py:48
  784.2 71.7 %reduce-scatter.2.cloned.1.call-done = bf16[32,512]{1,0:T(8,128)(2,1)} async-done(((bf16[32,8192]{1,0:T(8,128)(2,1)}), bf16[32,512]{1,0:T(8,128)(2,1)}) %reduce-scatter.2.cloned.1.call-update) | async-done | bytes 32784 | tf_op jit(solution)/shard_map/while/body/eval_jaxpr/reduce_scatter | solution.py:56
  890.2 71.7 %reduce-scatter.2.cloned.1.call-done = bf16[32,512]{1,0:T(8,128)(2,1)} async-done(((bf16[32,8192]{1,0:T(8,128)(2,1)}), bf16[32,512]{1,0:T(8,128)(2,1)}) %reduce-scatter.2.cloned.1.call-update) | async-done | bytes 32784 | tf_op jit(solution)/shard_map/while/body/eval_jaxpr/reduce_scatter | solution.py:56
  996.4 71.8 %reduce-scatter.2.cloned.1.call-done = bf16[32,512]{1,0:T(8,128)(2,1)} async-done(((bf16[32,8192]{1,0:T(8,128)(2,1)}), bf16[32,512]{1,0:T(8,128)(2,1)}) %reduce-scatter.2.cloned.1.call-update) | async-done | bytes 32784 | tf_op jit(solution)/shard_map/while/body/eval_jaxpr/reduce_scatter | solution.py:56
  1102.5 71.7 %reduce-scatter.2.cloned.1.call-done = bf16[32,512]{1,0:T(8,128)(2,1)} async-done(((bf16[32,8192]{1,0:T(8,128)(2,1)}), bf16[32,512]{1,0:T(8,128)(2,1)}) %reduce-scatter.2.cloned.1.call-update) | async-done | bytes 32784 | tf_op jit(solution)/shard_map/while/body/eval_jaxpr/reduce_scatter | solution.py:56
  1208.6 71.7 %reduce-scatter.2.cloned.1.call-done = bf16[32,512]{1,0:T(8,128)(2,1)} async-done(((bf16[32,8192]{1,0:T(8,128)(2,1)}), bf16[32,512]{1,0:T(8,128)(2,1)}) %reduce-scatter.2.cloned.1.call-update) | async-done | bytes 32784 | tf_op jit(solution)/shard_map/while/body/eval_jaxpr/reduce_scatter | solution.py:56
  1314.7 71.8 %reduce-scatter.2.cloned.1.call-done = bf16[32,512]{1,0:T(8,128)(2,1)} async-done(((bf16[32,8192]{1,0:T(8,128)(2,1)}), bf16[32,512]{1,0:T(8,128)(2,1)}) %reduce-scatter.2.cloned.1.call-update) | async-done | bytes 32784 | tf_op jit(solution)/shard_map/while/body/eval_jaxpr/reduce_scatter | solution.py:56
  1420.9 71.8 %reduce-scatter.2.cloned.1.call-done = bf16[32,512]{1,0:T(8,128)(2,1)} async-done(((bf16[32,8192]{1,0:T(8,128)(2,1)}), bf16[32,512]{1,0:T(8,128)(2,1)}) %reduce-scatter.2.cloned.1.call-update) | async-done | bytes 32784 | tf_op jit(solution)/shard_map/while/body/eval_jaxpr/reduce_scatter | solution.py:56
  1527.1 71.8 %reduce-scatter.2.cloned.1.call-done = bf16[32,512]{1,0:T(8,128)(2,1)} async-done(((bf16[32,8192]{1,0:T(8,128)(2,1)}), bf16[32,512]{1,0:T(8,128)(2,1)}) %reduce-scatter.2.cloned.1.call-update) | async-done | bytes 32784 | tf_op jit(solution)/shard_map/while/body/eval_jaxpr/reduce_scatter | solution.py:56
  1617.0 56.6 %all_to_all.30 = bf16[16,1,1024,128]{3,2,1,0:T(8,128)(2,1)} all-to-all(bf16[16,1,1024,128]{3,2,1,0:T(8,128)(2,1)S(1)} %copy.34), channel_id=1, replica_groups=mesh['section'=8,'kfac'=16] {'kfac'}, dimensions={0} | all-to-all | bytes 8388608 | tf_op jit(solution)/shard_map/all_to_all | solution.py:93
  1695.6 28.7 %copy.47 = bf16[1,1,1024,2048]{2,1,0,3:T(2,128)(2,1)} copy(bf16[1,1,1024,2048]{2,3,1,0:T(8,128)(2,1)S(1)} %bitcast.110) | data formatting | bytes 8388608 | tf_op jit(solution)/shard_map/reshape | solution.py:102
  1724.8 25.9 %reduce = bf16[2048,1024]{1,0:T(8,128)(2,1)} reduce(bf16[2048,1,1,1024]{3,2,1,0:T(2,128)(2,1)} %bitcast.103, bf16[]{:T(256)} %broadcast.22), dimensions={1,2}, to_apply=%bitcast.82.reduce_sub_computation | reduce | bytes 8388610
  1762.1 57.5 %all_to_all.31 = bf16[16,2,65536]{2,1,0:T(2,128)(2,1)} all-to-all(bf16[16,2,65536]{2,1,0:T(2,128)(2,1)} %reshape.52), channel_id=1, replica_groups=mesh['section'=8,'kfac'=16] {'kfac'}, dimensions={0} | all-to-all | bytes 8388608 | tf_op jit(solution)/shard_map/all_to_all | solution.py:103
  (204 shorter events, 502.8 us)
Async XLA Ops:
  8.9 104.2 %reduce-scatter.2.cloned.1.call-start = ((), (), s32[]{:S(2)}) async-start(), calls=%async_computation.3 | async-start | bytes 557056 | tf_op jit(solution)/shard_map/while/body/eval_jaxpr/reduce_scatter | solution.py:56
  113.9 3.1 collective-permute-start
  117.0 102.2 %reduce-scatter.2.cloned.1.call-start = ((), (), s32[]{:S(2)}) async-start(), calls=%async_computation.3 | async-start | bytes 557056 | tf_op jit(solution)/shard_map/while/body/eval_jaxpr/reduce_scatter | solution.py:56
  220.0 3.1 collective-permute-start
  223.1 102.2 %reduce-scatter.2.cloned.1.call-start = ((), (), s32[]{:S(2)}) async-start(), calls=%async_computation.3 | async-start | bytes 557056 | tf_op jit(solution)/shard_map/while/body/eval_jaxpr/reduce_scatter | solution.py:56
  326.1 3.1 collective-permute-start
  329.2 102.2 %reduce-scatter.2.cloned.1.call-start = ((), (), s32[]{:S(2)}) async-start(), calls=%async_computation.3 | async-start | bytes 557056 | tf_op jit(solution)/shard_map/while/body/eval_jaxpr/reduce_scatter | solution.py:56
  432.2 3.1 collective-permute-start
  435.3 102.2 %reduce-scatter.2.cloned.1.call-start = ((), (), s32[]{:S(2)}) async-start(), calls=%async_computation.3 | async-start | bytes 557056 | tf_op jit(solution)/shard_map/while/body/eval_jaxpr/reduce_scatter | solution.py:56
  538.3 3.1 collective-permute-start
  541.4 102.2 %reduce-scatter.2.cloned.1.call-start = ((), (), s32[]{:S(2)}) async-start(), calls=%async_computation.3 | async-start | bytes 557056 | tf_op jit(solution)/shard_map/while/body/eval_jaxpr/reduce_scatter | solution.py:56
  647.5 102.2 %reduce-scatter.2.cloned.1.call-start = ((), (), s32[]{:S(2)}) async-start(), calls=%async_computation.3 | async-start | bytes 557056 | tf_op jit(solution)/shard_map/while/body/eval_jaxpr/reduce_scatter | solution.py:56
  750.5 3.1 collective-permute-start
  753.6 102.2 %reduce-scatter.2.cloned.1.call-start = ((), (), s32[]{:S(2)}) async-start(), calls=%async_computation.3 | async-start | bytes 557056 | tf_op jit(solution)/shard_map/while/body/eval_jaxpr/reduce_scatter | solution.py:56
  856.6 3.1 collective-permute-start
  859.7 102.3 %reduce-scatter.2.cloned.1.call-start = ((), (), s32[]{:S(2)}) async-start(), calls=%async_computation.3 | async-start | bytes 557056 | tf_op jit(solution)/shard_map/while/body/eval_jaxpr/reduce_scatter | solution.py:56
  962.7 3.1 collective-permute-start
  965.8 102.3 %reduce-scatter.2.cloned.1.call-start = ((), (), s32[]{:S(2)}) async-start(), calls=%async_computation.3 | async-start | bytes 557056 | tf_op jit(solution)/shard_map/while/body/eval_jaxpr/reduce_scatter | solution.py:56
  1068.9 3.1 collective-permute-start
  1072.0 102.2 %reduce-scatter.2.cloned.1.call-start = ((), (), s32[]{:S(2)}) async-start(), calls=%async_computation.3 | async-start | bytes 557056 | tf_op jit(solution)/shard_map/while/body/eval_jaxpr/reduce_scatter | solution.py:56
  1178.1 102.2 %reduce-scatter.2.cloned.1.call-start = ((), (), s32[]{:S(2)}) async-start(), calls=%async_computation.3 | async-start | bytes 557056 | tf_op jit(solution)/shard_map/while/body/eval_jaxpr/reduce_scatter | solution.py:56
  1284.2 102.3 %reduce-scatter.2.cloned.1.call-start = ((), (), s32[]{:S(2)}) async-start(), calls=%async_computation.3 | async-start | bytes 557056 | tf_op jit(solution)/shard_map/while/body/eval_jaxpr/reduce_scatter | solution.py:56
  1390.4 102.3 %reduce-scatter.2.cloned.1.call-start = ((), (), s32[]{:S(2)}) async-start(), calls=%async_computation.3 | async-start | bytes 557056 | tf_op jit(solution)/shard_map/while/body/eval_jaxpr/reduce_scatter | solution.py:56
  1496.6 102.3 %reduce-scatter.2.cloned.1.call-start = ((), (), s32[]{:S(2)}) async-start(), calls=%async_computation.3 | async-start | bytes 557056 | tf_op jit(solution)/shard_map/while/body/eval_jaxpr/reduce_scatter | solution.py:56
  (25 other events, 1789.2 us)
Sparse Core Ops, SparseCore 0:
  40.6 72.4 reduce-scatter.1
  147.6 71.5 reduce-scatter.1
  253.7 71.5 reduce-scatter.1
  359.8 71.5 reduce-scatter.1
  466.0 71.5 reduce-scatter.1
  572.0 71.5 reduce-scatter.1
  678.2 71.5 reduce-scatter.1
  784.3 71.4 reduce-scatter.1
  890.3 71.5 reduce-scatter.1
  996.5 71.6 reduce-scatter.1
  1102.6 71.5 reduce-scatter.1
  1208.8 71.5 reduce-scatter.1
  1314.9 71.6 reduce-scatter.1
  1421.0 71.6 reduce-scatter.1
  1527.2 71.6 reduce-scatter.1
where the time goes:
time: 1860 us
  waiting for transfers between devices  1100 us (59%)
  blocking collectives  465 us (25%)
  matrix products  120 us (6%)
  local copies, waits for them, and re-layouts  83.4 us (4%)
  other arithmetic  50.7 us (3%)
  starting transfers between devices  19.5 us (1%)
    reduce_scatter x15, waiting for transfers between devices, one_tick(): lax.psum_scatter(partial_terms.astype(jnp.bfloat16), 'kfac', scatter_dime...  1080 us
    all_gather x15, blocking collectives, one_tick(): whole = lax.all_gather(shard, 'kfac', axis=1, tiled=True)  351 us
    all_to_all x1, blocking collectives, on_device(): lax.all_to_all(sendback, 'kfac', split_axis=3, concat_axis=0, tiled=True)  57.5 us
    all_to_all x1, blocking collectives, on_device(): lax.all_to_all(outgoing, 'kfac', split_axis=0, concat_axis=3, tiled=True)  56.6 us
  transfers between devices with their start and end apart: 30, of which 30 were waited for; matrix products, arithmetic and copies ran while one was open for 0% of the time, Pallas kernels for 0%

commit v1 on v0

v1 whole, which is shorter than its diff:
```python
import jax
import jax.numpy as jnp
from jax import lax
from jax.experimental import pallas as pl
from jax.experimental.pallas import tpu as pltpu
from jax.sharding import PartitionSpec as P

BF = jnp.bfloat16
F32 = jnp.float32
SIDE = 4
AXES = ("section", "kfac")


def silu_slope(values):
    sigmoid = jax.nn.sigmoid(values)
    return sigmoid * (1.0 + values * (1.0 - sigmoid))


def slot_numbers(owner_row):
    blocks = owner_row.shape[0]
    earlier = jnp.arange(blocks)[None, :] < jnp.arange(blocks)[:, None]
    shared = owner_row[None, :] == owner_row[:, None]
    return jnp.sum(jnp.logical_and(earlier, shared).astype(jnp.int32), axis=1)


def shift(block, rows, cols):
    route = []
    for row in range(SIDE):
        for col in range(SIDE):
            source = (row + rows) % SIDE * SIDE + (col + cols) % SIDE
            route.append((source, row * SIDE + col))
    return lax.ppermute(block, "kfac", route)


def shift_section(block, source_section, target_section, rows, cols):
    size = SIDE * SIDE
    route = []
    for row in range(SIDE):
        for col in range(SIDE):
            source = (row + rows) % SIDE * SIDE + (col + cols) % SIDE
            route.append((source_section * size + source, target_section * size + row * SIDE + col))
    return lax.ppermute(block, AXES, route)


def dot_nt(left, right):
    return lax.dot_general(left, right, (((1,), (1,)), ((), ())), preferred_element_type=F32)


def dot_nn(left, right):
    return lax.dot_general(left, right, (((1,), (0,)), ((), ())), preferred_element_type=F32)


def spread_kernel(slots_ref, left_ref, right_ref, out_ref):
    out_ref[...] = jnp.dot(
        left_ref[0], right_ref[...], preferred_element_type=F32
    ).astype(out_ref.dtype)


def spread(slots, left, right, block_count):
    _, height, depth = left.shape
    width = right.shape[1]
    return pl.pallas_call(
        spread_kernel,
        grid_spec=pltpu.PrefetchScalarGridSpec(
            num_scalar_prefetch=1,
            grid=(block_count,),
            in_specs=[
                pl.BlockSpec((1, height, depth), lambda b, slots: (slots[b], 0, 0)),
                pl.BlockSpec((depth, width), lambda b, slots: (0, 0)),
            ],
            out_specs=pl.BlockSpec((height, width), lambda b, slots: (b, 0)),
        ),
        out_shape=jax.ShapeDtypeStruct((block_count * height, width), BF),
        compiler_params=pltpu.CompilerParams(vmem_limit_bytes=16 * 1024 * 1024),
        cost_estimate=pl.CostEstimate(
            flops=2 * block_count * height * depth * width,
            bytes_accessed=2 * block_count * height * (depth + width),
            transcendentals=0,
        ),
    )(slots, left, right)


def on_device(
    top_cotangent, inputs, proj_weight, return_weight, owners, input_inverses, output_inverses
):
    section_count = lax.axis_size("section")
    section_here = lax.axis_index("section")
    kfac_here = lax.axis_index("kfac")
    row, col = kfac_here // SIDE, kfac_here % SIDE
    micro, per_micro, shard_width = top_cotangent.shape
    tokens = micro * per_micro
    x = inputs[0].reshape(tokens, -1)
    weight = proj_weight[0]
    returning = return_weight[0]
    width, stripe = weight.shape
    quarter = width // SIDE
    block_width = input_inverses.shape[2]
    block_count = width // block_width
    group_count = output_inverses.shape[1]

    back_parts = [lax.dynamic_slice(returning, (0, row * quarter), (stripe, quarter))]
    proj_parts = [lax.dynamic_slice(weight, (row * quarter, 0), (quarter, stripe))]
    for rows in range(1, SIDE):
        there = (row - rows) % SIDE
        back_parts.append(
            shift(lax.dynamic_slice(returning, (0, there * quarter), (stripe, quarter)), rows, 0)
        )
    top = top_cotangent.reshape(tokens, shard_width)
    incoming = [top] + [shift(top, 0, cols) for cols in range(1, SIDE)]
    for rows in range(1, SIDE):
        there = (row - rows) % SIDE
        proj_parts.append(
            shift(lax.dynamic_slice(weight, (there * quarter, 0), (quarter, stripe)), rows, 0)
        )
    slopes_here = silu_slope(dot_nn(x, weight))
    slope_parts = [slopes_here] + [shift(slopes_here, rows, 0) for rows in range(1, SIDE)]

    place = [(row + rows) % SIDE * stripe for rows in range(SIDE)]
    block = SIDE * stripe
    back_weight = jnp.zeros((block, quarter), BF)
    proj_block = jnp.zeros((quarter, block), BF)
    factor = jnp.zeros((tokens, block), F32)
    for rows in range(SIDE):
        back_weight = lax.dynamic_update_slice(back_weight, back_parts[rows], (place[rows], 0))
        proj_block = lax.dynamic_update_slice(proj_block, proj_parts[rows], (0, place[rows]))
        factor = lax.dynamic_update_slice(factor, slope_parts[rows], (0, place[rows]))
    back_rel = [
        lax.dynamic_slice(back_weight, (0, (col + cols) % SIDE * shard_width), (block, shard_width))
        for cols in range(SIDE)
    ]
    proj_rel = [
        lax.dynamic_slice(proj_block, ((col - cols) % SIDE * shard_width, 0), (shard_width, block))
        for cols in range(SIDE)
    ]

    targets = owners[0] + slot_numbers(owners[0])
    mine = targets == kfac_here
    block_here = jnp.sum(jnp.where(mine, jnp.arange(block_count, dtype=jnp.int32), 0))
    x_block = lax.dynamic_slice(x, (0, block_here * block_width), (tokens, block_width))
    left_here = dot_nt(input_inverses[0, 0], x_block).astype(BF)
    left_all = lax.all_gather(left_here, "kfac", axis=0)

    group_here = kfac_here * stripe // block_width
    per_group = SIDE // group_count
    out_cols = lax.dynamic_slice(
        output_inverses[0],
        (group_here, 0, kfac_here * stripe % block_width),
        (1, block_width, stripe),
    ).reshape(per_group, SIDE, stripe, stripe)
    out_rel = [
        lax.dynamic_index_in_dim(out_cols, (col + cols) % SIDE, 1, keepdims=False).reshape(
            per_group * stripe, stripe
        )
        for cols in range(SIDE)
    ]

    outputs = jnp.zeros((tokens, shard_width), BF)
    slope_saved = jnp.zeros((tokens, per_group * stripe), BF)
    for section in range(section_count - 1, -1, -1):
        active = section_here == section
        back = sum(dot_nt(c, u) for c, u in zip(incoming, back_rel))
        back_sent = back.astype(BF)
        for rows in range(1, SIDE):
            back = back + shift_section(back_sent, section, section, rows, 0).astype(F32)
        slope = (back * factor).astype(BF)
        slope_group = lax.dynamic_slice(
            slope, (0, group_here * per_group * stripe), (tokens, per_group * stripe)
        )
        slope_saved = jnp.where(active, slope_group, slope_saved)
        summed = incoming[0].astype(F32) + dot_nt(slope, proj_rel[0])
        for cols in range(1, SIDE):
            part = dot_nt(slope, proj_rel[cols]).astype(BF)
            summed = summed + shift_section(part, section, section, 0, cols).astype(F32)
        updated = summed.astype(BF)
        outputs = jnp.where(active, updated, outputs)
        if section > 0:
            incoming = [
                shift_section(updated, section, section - 1, 0, cols) for cols in range(SIDE)
            ]

    right = dot_nn(slope_saved, out_rel[0])
    for cols in range(1, SIDE):
        right = right + dot_nn(shift(slope_saved, 0, cols), out_rel[cols])
    result = spread(targets, left_all, right.astype(BF), block_count)
    return outputs.reshape(1, micro, per_micro, shard_width), result[None]


def solution(mesh):
    return jax.shard_map(
        on_device,
        mesh=mesh,
        in_specs=(
            P(None, None, "kfac"),
            P("section", None, None, None),
            P("section", None, "kfac"),
            P("section", "kfac", None),
            P("section", None),
            P("section", "kfac", None, None),
            P("section", None, None, None),
        ),
        out_specs=(P("section", None, None, "kfac"), P("section", None, "kfac")),
        check_vma=False,
    )
```

time: 1860 us -> 850 us (0.46)
  waiting for transfers between devices: 1100 us -> 98.9 us
  starting transfers between devices: 19.5 us -> 581 us
  blocking collectives: 465 us -> 0 us
  local copies, waits for them, and re-layouts: 83.4 us -> 34.6 us
  other arithmetic: 50.7 us -> 7.23 us
  matrix products: 120 us -> 101 us
    reduce_scatter x15 -> x0, waiting for transfers between devices: 1080 us -> none  [one_tick(): lax.psum_scatter(partial_terms.astype(jnp.bfloat16), 'kfac', scatter_dime...]
    ppermute x15 -> x91, starting transfers between devices: 19.4 us -> 581 us  [the longest x76 544 us: shift_section(): return lax.ppermute(block, AXES, route)]
    all_gather x15 -> x0, blocking collectives: 351 us -> none  [one_tick(): whole = lax.all_gather(shard, 'kfac', axis=1, tiled=True)]
    all_to_all x2 -> x0, blocking collectives: 114 us -> none  [the longest x1 57.5 us: on_device(): lax.all_to_all(sendback, 'kfac', split_axis=3, concat_axis=0, tiled=True)]
    ppermute x15 -> x91, waiting for transfers between devices: 27 us -> 98.9 us  [the longest x76 84.5 us: shift_section(): return lax.ppermute(block, AXES, route)]
    reshape x3 -> x0, local copies, waits for them, and re-layouts: 34.3 us -> none  [the longest x1 28.7 us: on_device(): right_product.reshape(1, slot_count, block_width, group_count * block_width)]
    unnamed x13 -> x40, local copies, waits for them, and re-layouts: 34 us -> 3.47 us
    unnamed x1 -> x0, other arithmetic: 25.9 us -> none
  transfers between devices with their start and end apart: 30 -> 92, of which waited for: 30 -> 7; matrix products, arithmetic and copies ran while one was open for 0% -> 12% of each run, Pallas kernels for 0% -> 0%
where the time goes in v1:
time: 850 us; the launch traced here: 845 us
  starting transfers between devices  581 us (68%)
  matrix products  101 us (12%)
  waiting for transfers between devices  98.9 us (12%)
  local copies, waits for them, and re-layouts  34.6 us (4%)
  between operations  16.9 us (2%)
    ppermute x76, starting transfers between devices, shift_section(): return lax.ppermute(block, AXES, route)  544 us
    dot_general x65, matrix products, dot_nt(): lax.dot_general(left, right, (((1,), (1,)), ((), ())), preferred_element_...  94.8 us
    ppermute x76, waiting for transfers between devices, shift_section(): return lax.ppermute(block, AXES, route)  84.5 us
    ppermute x15, starting transfers between devices, shift(): return lax.ppermute(block, 'kfac', route)  37.4 us
  transfers between devices with their start and end apart: 92, of which 7 were waited for; matrix products, arithmetic and copies ran while one was open for 12% of the time, Pallas kernels for 0%

profile of v1, /device:TPU:0, one launch (start us, length us, event | category | flops | bytes accessed | tf_op | source)
XLA Modules:
  0.0 844.7 jit_solution(4088516170508178675)
XLA Ops:
  116.1 11.9 %collective-permute-start.17 = (bf16[256,512]{1,0:T(8,128)(2,1)S(1)}, bf16[256,512]{1,0:T(8,128)(2,1)S(1)}, u32[]{:S(2)}, u32[]{:S(2)}) collective-permute-start(bf16[256,512]{1,0:T(8,128)(2,1)S(1)} %convolution_convert_fusion.21), channel_id=1, source_target_pairs={{115,112},{112,113},{113,114},{114,115},{119,116},{116,117},{117,1... | collective-permute-start | bytes 786440 | tf_op jit(solution)/shard_map/ppermute | solution.py:42
  152.1 14.5 %collective-permute-start.21 = (bf16[256,512]{1,0:T(8,128)(2,1)S(1)}, bf16[256,512]{1,0:T(8,128)(2,1)S(1)}, u32[]{:S(2)}, u32[]{:S(2)}) collective-permute-start(bf16[256,512]{1,0:T(8,128)(2,1)S(1)} %fusion.30), channel_id=1, source_target_pairs={{115,96},{112,97},{113,98},{114,99},{119,100},{116,101},{117,102},... | collective-permute-start | bytes 786440 | tf_op jit(solution)/shard_map/ppermute | solution.py:42
  222.1 10.3 %collective-permute-start.22 = (bf16[256,512]{0,1:T(8,128)(2,1)S(1)}, bf16[256,512]{0,1:T(8,128)(2,1)S(1)}, u32[]{:S(2)}, u32[]{:S(2)}) collective-permute-start(bf16[256,512]{0,1:T(8,128)(2,1)S(1)} %get-tuple-element.18), channel_id=1, source_target_pairs={{100,96},{101,97},{102,98},{103,99},{104,100},{105,101},{106,102},... | collective-permute-start | bytes 786440 | tf_op jit(solution)/shard_map/ppermute | solution.py:42
  236.8 15.5 %collective-permute-start.27 = (bf16[256,512]{1,0:T(8,128)(2,1)S(1)}, bf16[256,512]{1,0:T(8,128)(2,1)S(1)}, u32[]{:S(2)}, u32[]{:S(2)}) collective-permute-start(bf16[256,512]{1,0:T(8,128)(2,1)S(1)} %convolution_convert_fusion.18), channel_id=1, source_target_pairs={{99,96},{96,97},{97,98},{98,99},{103,100},{100,101},{101,102},{102... | collective-permute-start | bytes 786440 | tf_op jit(solution)/shard_map/ppermute | solution.py:42
  274.3 14.2 %collective-permute-start.31 = (bf16[256,512]{1,0:T(8,128)(2,1)S(1)}, bf16[256,512]{1,0:T(8,128)(2,1)S(1)}, u32[]{:S(2)}, u32[]{:S(2)}) collective-permute-start(bf16[256,512]{1,0:T(8,128)(2,1)S(1)} %add_convert_fusion.6), channel_id=1, source_target_pairs={{99,80},{96,81},{97,82},{98,83},{103,84},{100,85},{101,86},{102,87... | collective-permute-start | bytes 786440 | tf_op jit(solution)/shard_map/ppermute | solution.py:42
  324.7 11.1 %collective-permute-start.34 = (bf16[256,512]{0,1:T(8,128)(2,1)S(1)}, bf16[256,512]{0,1:T(8,128)(2,1)S(1)}, u32[]{:S(2)}, u32[]{:S(2)}) collective-permute-start(bf16[256,512]{0,1:T(8,128)(2,1)S(1)} %get-tuple-element.20), channel_id=1, source_target_pairs={{92,80},{93,81},{94,82},{95,83},{80,84},{81,85},{82,86},{83,87},{8... | collective-permute-start | bytes 786440 | tf_op jit(solution)/shard_map/ppermute | solution.py:42
  362.4 15.1 %collective-permute-start.37 = (bf16[256,512]{1,0:T(8,128)(2,1)}, bf16[256,512]{1,0:T(8,128)(2,1)}, u32[]{:S(2)}, u32[]{:S(2)}) collective-permute-start(bf16[256,512]{1,0:T(8,128)(2,1)} %convolution_convert_fusion.15), channel_id=1, source_target_pairs={{83,80},{80,81},{81,82},{82,83},{87,84},{84,85},{85,86},{86,87},{9... | collective-permute-start | bytes 786440 | tf_op jit(solution)/shard_map/ppermute | solution.py:42
  377.5 10.2 %collective-permute-start.36 = (bf16[256,512]{1,0:T(8,128)(2,1)}, bf16[256,512]{1,0:T(8,128)(2,1)}, u32[]{:S(2)}, u32[]{:S(2)}) collective-permute-start(bf16[256,512]{1,0:T(8,128)(2,1)} %convolution_convert_fusion.16), channel_id=1, source_target_pairs={{82,80},{83,81},{80,82},{81,83},{86,84},{87,85},{84,86},{85,87},{9... | collective-permute-start | bytes 786440 | tf_op jit(solution)/shard_map/ppermute | solution.py:42
  387.8 10.3 %collective-permute-start.35 = (bf16[256,512]{1,0:T(8,128)(2,1)}, bf16[256,512]{1,0:T(8,128)(2,1)}, u32[]{:S(2)}, u32[]{:S(2)}) collective-permute-start(bf16[256,512]{1,0:T(8,128)(2,1)} %convolution_convert_fusion.17), channel_id=1, source_target_pairs={{81,80},{82,81},{83,82},{80,83},{85,84},{86,85},{87,86},{84,87},{8... | collective-permute-start | bytes 786440 | tf_op jit(solution)/shard_map/ppermute | solution.py:42
  402.8 12.1 %collective-permute-start.41 = (bf16[256,512]{1,0:T(8,128)(2,1)}, bf16[256,512]{1,0:T(8,128)(2,1)}, u32[]{:S(2)}, u32[]{:S(2)}) collective-permute-start(bf16[256,512]{1,0:T(8,128)(2,1)} %add_convert_fusion.5), channel_id=1, source_target_pairs={{83,64},{80,65},{81,66},{82,67},{87,68},{84,69},{85,70},{86,71},{9... | collective-permute-start | bytes 786440 | tf_op jit(solution)/shard_map/ppermute | solution.py:42
  415.0 10.7 %collective-permute-start.40 = (bf16[256,512]{1,0:T(8,128)(2,1)}, bf16[256,512]{1,0:T(8,128)(2,1)}, u32[]{:S(2)}, u32[]{:S(2)}) collective-permute-start(bf16[256,512]{1,0:T(8,128)(2,1)} %add_convert_fusion.5), channel_id=1, source_target_pairs={{82,64},{83,65},{80,66},{81,67},{86,68},{87,69},{84,70},{85,71},{9... | collective-permute-start | bytes 786440 | tf_op jit(solution)/shard_map/ppermute | solution.py:42
  463.9 10.2 %collective-permute-start.43 = (bf16[256,512]{0,1:T(8,128)(2,1)S(1)}, bf16[256,512]{0,1:T(8,128)(2,1)S(1)}, u32[]{:S(2)}, u32[]{:S(2)}) collective-permute-start(bf16[256,512]{0,1:T(8,128)(2,1)S(1)} %get-tuple-element.22), channel_id=1, source_target_pairs={{72,64},{73,65},{74,66},{75,67},{76,68},{77,69},{78,70},{79,71},{6... | collective-permute-start | bytes 786440 | tf_op jit(solution)/shard_map/ppermute | solution.py:42
  474.0 10.2 %collective-permute-start.42 = (bf16[256,512]{0,1:T(8,128)(2,1)S(1)}, bf16[256,512]{0,1:T(8,128)(2,1)S(1)}, u32[]{:S(2)}, u32[]{:S(2)}) collective-permute-start(bf16[256,512]{0,1:T(8,128)(2,1)S(1)} %get-tuple-element.22), channel_id=1, source_target_pairs={{68,64},{69,65},{70,66},{71,67},{72,68},{73,69},{74,70},{75,71},{7... | collective-permute-start | bytes 786440 | tf_op jit(solution)/shard_map/ppermute | solution.py:42
  488.6 21.3 %collective-permute-start.47 = (bf16[256,512]{1,0:T(8,128)(2,1)S(1)}, bf16[256,512]{1,0:T(8,128)(2,1)S(1)}, u32[]{:S(2)}, u32[]{:S(2)}) collective-permute-start(bf16[256,512]{1,0:T(8,128)(2,1)S(1)} %convolution_convert_fusion.12), channel_id=1, source_target_pairs={{67,64},{64,65},{65,66},{66,67},{71,68},{68,69},{69,70},{70,71},{7... | collective-permute-start | bytes 786440 | tf_op jit(solution)/shard_map/ppermute | solution.py:42
  509.9 10.2 %collective-permute-start.46 = (bf16[256,512]{1,0:T(8,128)(2,1)S(1)}, bf16[256,512]{1,0:T(8,128)(2,1)S(1)}, u32[]{:S(2)}, u32[]{:S(2)}) collective-permute-start(bf16[256,512]{1,0:T(8,128)(2,1)S(1)} %convolution_convert_fusion.13), channel_id=1, source_target_pairs={{66,64},{67,65},{64,66},{65,67},{70,68},{71,69},{68,70},{69,71},{7... | collective-permute-start | bytes 786440 | tf_op jit(solution)/shard_map/ppermute | solution.py:42
  520.1 10.2 %collective-permute-start.45 = (bf16[256,512]{1,0:T(8,128)(2,1)S(1)}, bf16[256,512]{1,0:T(8,128)(2,1)S(1)}, u32[]{:S(2)}, u32[]{:S(2)}) collective-permute-start(bf16[256,512]{1,0:T(8,128)(2,1)S(1)} %convolution_convert_fusion.14), channel_id=1, source_target_pairs={{65,64},{66,65},{67,66},{64,67},{69,68},{70,69},{71,70},{68,71},{7... | collective-permute-start | bytes 786440 | tf_op jit(solution)/shard_map/ppermute | solution.py:42
  531.9 14.2 %collective-permute-start.51 = (bf16[256,512]{1,0:T(8,128)(2,1)S(1)}, bf16[256,512]{1,0:T(8,128)(2,1)S(1)}, u32[]{:S(2)}, u32[]{:S(2)}) collective-permute-start(bf16[256,512]{1,0:T(8,128)(2,1)S(1)} %add_convert_fusion.4), channel_id=1, source_target_pairs={{67,48},{64,49},{65,50},{66,51},{71,52},{68,53},{69,54},{70,55},{7... | collective-permute-start | bytes 786440 | tf_op jit(solution)/shard_map/ppermute | solution.py:42
  546.2 10.2 %collective-permute-start.50 = (bf16[256,512]{1,0:T(8,128)(2,1)S(1)}, bf16[256,512]{1,0:T(8,128)(2,1)S(1)}, u32[]{:S(2)}, u32[]{:S(2)}) collective-permute-start(bf16[256,512]{1,0:T(8,128)(2,1)S(1)} %add_convert_fusion.4), channel_id=1, source_target_pairs={{66,48},{67,49},{64,50},{65,51},{70,52},{71,53},{68,54},{69,55},{7... | collective-permute-start | bytes 786440 | tf_op jit(solution)/shard_map/ppermute | solution.py:42
  556.4 10.2 %collective-permute-start.49 = (bf16[256,512]{1,0:T(8,128)(2,1)S(1)}, bf16[256,512]{1,0:T(8,128)(2,1)S(1)}, u32[]{:S(2)}, u32[]{:S(2)}) collective-permute-start(bf16[256,512]{1,0:T(8,128)(2,1)S(1)} %add_convert_fusion.4), channel_id=1, source_target_pairs={{65,48},{66,49},{67,50},{64,51},{69,52},{70,53},{71,54},{68,55},{7... | collective-permute-start | bytes 786440 | tf_op jit(solution)/shard_map/ppermute | solution.py:42
  566.6 10.2 %collective-permute-start.48 = (bf16[256,512]{1,0:T(8,128)(2,1)S(1)}, bf16[256,512]{1,0:T(8,128)(2,1)S(1)}, u32[]{:S(2)}, u32[]{:S(2)}) collective-permute-start(bf16[256,512]{1,0:T(8,128)(2,1)S(1)} %add_convert_fusion.4), channel_id=1, source_target_pairs={{64,48},{65,49},{66,50},{67,51},{68,52},{69,53},{70,54},{71,55},{7... | collective-permute-start | bytes 786440 | tf_op jit(solution)/shard_map/ppermute | solution.py:42
  582.4 10.2 %collective-permute-start.54 = (bf16[256,512]{0,1:T(8,128)(2,1)S(1)}, bf16[256,512]{0,1:T(8,128)(2,1)S(1)}, u32[]{:S(2)}, u32[]{:S(2)}) collective-permute-start(bf16[256,512]{0,1:T(8,128)(2,1)S(1)} %get-tuple-element.24), channel_id=1, source_target_pairs={{60,48},{61,49},{62,50},{63,51},{48,52},{49,53},{50,54},{51,55},{5... | collective-permute-start | bytes 786440 | tf_op jit(solution)/shard_map/ppermute | solution.py:42
  616.1 12.8 %collective-permute-start.57 = (bf16[256,512]{1,0:T(8,128)(2,1)S(1)}, bf16[256,512]{1,0:T(8,128)(2,1)S(1)}, u32[]{:S(2)}, u32[]{:S(2)}) collective-permute-start(bf16[256,512]{1,0:T(8,128)(2,1)S(1)} %convolution_convert_fusion.9), channel_id=1, source_target_pairs={{51,48},{48,49},{49,50},{50,51},{55,52},{52,53},{53,54},{54,55},{5... | collective-permute-start | bytes 786440 | tf_op jit(solution)/shard_map/ppermute | solution.py:42
  692.0 75.8 %collective-permute-done.81 = bf16[256,512]{1,0:T(8,128)(2,1)S(1)} collective-permute-done((bf16[256,512]{1,0:T(8,128)(2,1)S(1)}, bf16[256,512]{1,0:T(8,128)(2,1)S(1)}, u32[]{:S(2)}, u32[]{:S(2)}) %collective-permute-start.81) | collective-permute-done | bytes 262176 | tf_op jit(solution)/shard_map/ppermute | solution.py:42
  817.7 11.9 %copy.70 = bf16[16384,256]{1,0:T(8,128)(2,1)} copy(bf16[16384,256]{0,1:T(8,128)(2,1)} %all-gather.3.cloned.1.call-done) | data formatting | bytes 16777216 | tf_op jit(solution)/shard_map/all_gather | solution.py:141
  (309 shorter events, 474.4 us)
Async XLA Ops:
  7.2 810.5 %all-gather.3.cloned.1.call-start = ((), (), s32[]{:S(2)}) async-start(), calls=%async_computation | async-start | bytes 8912896 | tf_op jit(solution)/shard_map/all_gather | solution.py:141
  12.5 35.3 %collective-permute-start.9 = (f32[256,128]{0,1:T(8,128)}, f32[256,128]{0,1:T(8,128)S(1)}, u32[]{:S(2)}, u32[]{:S(2)}) collective-permute-start(f32[256,128]{0,1:T(8,128)} %get-tuple-element.15), channel_id=1, source_target_pairs={{4,0},{5,1},{6,2},{7,3},{8,4},{9,5},{10,6},{11,7},{12,8},{13,9},{1... | collective-permute-start | bytes 393224 | tf_op jit(solution)/shard_map/ppermute | solution.py:32
  32.7 43.8 %collective-permute-start.5 = (bf16[256,512]{1,0:T(8,128)(2,1)S(1)}, bf16[256,512]{1,0:T(8,128)(2,1)S(1)}, u32[]{:S(2)}, u32[]{:S(2)}) collective-permute-start(bf16[256,512]{1,0:T(8,128)(2,1)S(1)} %bitcast.125), channel_id=1, source_target_pairs={{3,0},{0,1},{1,2},{2,3},{7,4},{4,5},{5,6},{6,7},{11,8},{8,9},{9,10... | collective-permute-start | bytes 786440 | tf_op jit(solution)/shard_map/ppermute | solution.py:32
  64.4 37.5 %collective-permute-start.12 = (bf16[2048,128]{1,0:T(8,128)(2,1)}, bf16[2048,128]{1,0:T(8,128)(2,1)S(1)}, u32[]{:S(2)}, u32[]{:S(2)}) collective-permute-start(bf16[2048,128]{1,0:T(8,128)(2,1)} %get-tuple-element.5), channel_id=1, source_target_pairs={{4,0},{5,1},{6,2},{7,3},{8,4},{9,5},{10,6},{11,7},{12,8},{13,9},{1... | collective-permute-start | bytes 1572872 | tf_op jit(solution)/shard_map/ppermute | solution.py:32
  73.9 38.9 %collective-permute-start.13 = (bf16[2048,128]{1,0:T(8,128)(2,1)}, bf16[2048,128]{1,0:T(8,128)(2,1)S(1)}, u32[]{:S(2)}, u32[]{:S(2)}) collective-permute-start(bf16[2048,128]{1,0:T(8,128)(2,1)} %get-tuple-element.6), channel_id=1, source_target_pairs={{8,0},{9,1},{10,2},{11,3},{12,4},{13,5},{14,6},{15,7},{0,8},{1,9},... | collective-permute-start | bytes 1572872 | tf_op jit(solution)/shard_map/ppermute | solution.py:32
  76.5 37.1 %collective-permute-start.14 = (bf16[2048,128]{1,0:T(8,128)(2,1)}, bf16[2048,128]{1,0:T(8,128)(2,1)S(1)}, u32[]{:S(2)}, u32[]{:S(2)}) collective-permute-start(bf16[2048,128]{1,0:T(8,128)(2,1)} %get-tuple-element.4), channel_id=1, source_target_pairs={{12,0},{13,1},{14,2},{15,3},{0,4},{1,5},{2,6},{3,7},{4,8},{5,9},{6... | collective-permute-start | bytes 1572872 | tf_op jit(solution)/shard_map/ppermute | solution.py:32
  82.0 32.5 %collective-permute-start.8 = (bf16[256,512]{0,1:T(8,128)(2,1)S(1)}, bf16[256,512]{0,1:T(8,128)(2,1)S(1)}, u32[]{:S(2)}, u32[]{:S(2)}) collective-permute-start(bf16[256,512]{0,1:T(8,128)(2,1)S(1)} %get-tuple-element.16), channel_id=1, source_target_pairs={{124,112},{125,113},{126,114},{127,115},{112,116},{113,117},{114,1... | collective-permute-start | bytes 786440 | tf_op jit(solution)/shard_map/ppermute | solution.py:42
  116.1 34.5 %collective-permute-start.17 = (bf16[256,512]{1,0:T(8,128)(2,1)S(1)}, bf16[256,512]{1,0:T(8,128)(2,1)S(1)}, u32[]{:S(2)}, u32[]{:S(2)}) collective-permute-start(bf16[256,512]{1,0:T(8,128)(2,1)S(1)} %convolution_convert_fusion.21), channel_id=1, source_target_pairs={{115,112},{112,113},{113,114},{114,115},{119,116},{116,117},{117,1... | collective-permute-start | bytes 786440 | tf_op jit(solution)/shard_map/ppermute | solution.py:42
  152.1 44.3 %collective-permute-start.21 = (bf16[256,512]{1,0:T(8,128)(2,1)S(1)}, bf16[256,512]{1,0:T(8,128)(2,1)S(1)}, u32[]{:S(2)}, u32[]{:S(2)}) collective-permute-start(bf16[256,512]{1,0:T(8,128)(2,1)S(1)} %fusion.30), channel_id=1, source_target_pairs={{115,96},{112,97},{113,98},{114,99},{119,100},{116,101},{117,102},... | collective-permute-start | bytes 786440 | tf_op jit(solution)/shard_map/ppermute | solution.py:42
  236.8 37.2 %collective-permute-start.27 = (bf16[256,512]{1,0:T(8,128)(2,1)S(1)}, bf16[256,512]{1,0:T(8,128)(2,1)S(1)}, u32[]{:S(2)}, u32[]{:S(2)}) collective-permute-start(bf16[256,512]{1,0:T(8,128)(2,1)S(1)} %convolution_convert_fusion.18), channel_id=1, source_target_pairs={{99,96},{96,97},{97,98},{98,99},{103,100},{100,101},{101,102},{102... | collective-permute-start | bytes 786440 | tf_op jit(solution)/shard_map/ppermute | solution.py:42
  274.3 44.8 %collective-permute-start.31 = (bf16[256,512]{1,0:T(8,128)(2,1)S(1)}, bf16[256,512]{1,0:T(8,128)(2,1)S(1)}, u32[]{:S(2)}, u32[]{:S(2)}) collective-permute-start(bf16[256,512]{1,0:T(8,128)(2,1)S(1)} %add_convert_fusion.6), channel_id=1, source_target_pairs={{99,80},{96,81},{97,82},{98,83},{103,84},{100,85},{101,86},{102,87... | collective-permute-start | bytes 786440 | tf_op jit(solution)/shard_map/ppermute | solution.py:42
  288.5 31.9 %collective-permute-start.30 = (bf16[256,512]{1,0:T(8,128)(2,1)S(1)}, bf16[256,512]{1,0:T(8,128)(2,1)S(1)}, u32[]{:S(2)}, u32[]{:S(2)}) collective-permute-start(bf16[256,512]{1,0:T(8,128)(2,1)S(1)} %add_convert_fusion.6), channel_id=1, source_target_pairs={{98,80},{99,81},{96,82},{97,83},{102,84},{103,85},{100,86},{101,87... | collective-permute-start | bytes 786440 | tf_op jit(solution)/shard_map/ppermute | solution.py:42
  324.7 31.2 %collective-permute-start.34 = (bf16[256,512]{0,1:T(8,128)(2,1)S(1)}, bf16[256,512]{0,1:T(8,128)(2,1)S(1)}, u32[]{:S(2)}, u32[]{:S(2)}) collective-permute-start(bf16[256,512]{0,1:T(8,128)(2,1)S(1)} %get-tuple-element.20), channel_id=1, source_target_pairs={{92,80},{93,81},{94,82},{95,83},{80,84},{81,85},{82,86},{83,87},{8... | collective-permute-start | bytes 786440 | tf_op jit(solution)/shard_map/ppermute | solution.py:42
  362.4 38.3 %collective-permute-start.37 = (bf16[256,512]{1,0:T(8,128)(2,1)}, bf16[256,512]{1,0:T(8,128)(2,1)}, u32[]{:S(2)}, u32[]{:S(2)}) collective-permute-start(bf16[256,512]{1,0:T(8,128)(2,1)} %convolution_convert_fusion.15), channel_id=1, source_target_pairs={{83,80},{80,81},{81,82},{82,83},{87,84},{84,85},{85,86},{86,87},{9... | collective-permute-start | bytes 786440 | tf_op jit(solution)/shard_map/ppermute | solution.py:42
  402.8 45.3 %collective-permute-start.41 = (bf16[256,512]{1,0:T(8,128)(2,1)}, bf16[256,512]{1,0:T(8,128)(2,1)}, u32[]{:S(2)}, u32[]{:S(2)}) collective-permute-start(bf16[256,512]{1,0:T(8,128)(2,1)} %add_convert_fusion.5), channel_id=1, source_target_pairs={{83,64},{80,65},{81,66},{82,67},{87,68},{84,69},{85,70},{86,71},{9... | collective-permute-start | bytes 786440 | tf_op jit(solution)/shard_map/ppermute | solution.py:42
  415.0 34.7 %collective-permute-start.40 = (bf16[256,512]{1,0:T(8,128)(2,1)}, bf16[256,512]{1,0:T(8,128)(2,1)}, u32[]{:S(2)}, u32[]{:S(2)}) collective-permute-start(bf16[256,512]{1,0:T(8,128)(2,1)} %add_convert_fusion.5), channel_id=1, source_target_pairs={{82,64},{83,65},{80,66},{81,67},{86,68},{87,69},{84,70},{85,71},{9... | collective-permute-start | bytes 786440 | tf_op jit(solution)/shard_map/ppermute | solution.py:42
  488.6 43.1 %collective-permute-start.47 = (bf16[256,512]{1,0:T(8,128)(2,1)S(1)}, bf16[256,512]{1,0:T(8,128)(2,1)S(1)}, u32[]{:S(2)}, u32[]{:S(2)}) collective-permute-start(bf16[256,512]{1,0:T(8,128)(2,1)S(1)} %convolution_convert_fusion.12), channel_id=1, source_target_pairs={{67,64},{64,65},{65,66},{66,67},{71,68},{68,69},{69,70},{70,71},{7... | collective-permute-start | bytes 786440 | tf_op jit(solution)/shard_map/ppermute | solution.py:42
  531.9 44.9 %collective-permute-start.51 = (bf16[256,512]{1,0:T(8,128)(2,1)S(1)}, bf16[256,512]{1,0:T(8,128)(2,1)S(1)}, u32[]{:S(2)}, u32[]{:S(2)}) collective-permute-start(bf16[256,512]{1,0:T(8,128)(2,1)S(1)} %add_convert_fusion.4), channel_id=1, source_target_pairs={{67,48},{64,49},{65,50},{66,51},{71,52},{68,53},{69,54},{70,55},{7... | collective-permute-start | bytes 786440 | tf_op jit(solution)/shard_map/ppermute | solution.py:42
  546.2 32.0 %collective-permute-start.50 = (bf16[256,512]{1,0:T(8,128)(2,1)S(1)}, bf16[256,512]{1,0:T(8,128)(2,1)S(1)}, u32[]{:S(2)}, u32[]{:S(2)}) collective-permute-start(bf16[256,512]{1,0:T(8,128)(2,1)S(1)} %add_convert_fusion.4), channel_id=1, source_target_pairs={{66,48},{67,49},{64,50},{65,51},{70,52},{71,53},{68,54},{69,55},{7... | collective-permute-start | bytes 786440 | tf_op jit(solution)/shard_map/ppermute | solution.py:42
  616.1 33.6 %collective-permute-start.57 = (bf16[256,512]{1,0:T(8,128)(2,1)S(1)}, bf16[256,512]{1,0:T(8,128)(2,1)S(1)}, u32[]{:S(2)}, u32[]{:S(2)}) collective-permute-start(bf16[256,512]{1,0:T(8,128)(2,1)S(1)} %convolution_convert_fusion.9), channel_id=1, source_target_pairs={{51,48},{48,49},{49,50},{50,51},{55,52},{52,53},{53,54},{54,55},{5... | collective-permute-start | bytes 786440 | tf_op jit(solution)/shard_map/ppermute | solution.py:42
  686.8 81.0 %collective-permute-start.81 = (bf16[256,512]{1,0:T(8,128)(2,1)S(1)}, bf16[256,512]{1,0:T(8,128)(2,1)S(1)}, u32[]{:S(2)}, u32[]{:S(2)}) collective-permute-start(bf16[256,512]{1,0:T(8,128)(2,1)S(1)} %add_convert_fusion.1), channel_id=1, source_target_pairs={{19,0},{16,1},{17,2},{18,3},{23,4},{20,5},{21,6},{22,7},{27,8},{24... | collective-permute-start | bytes 786440 | tf_op jit(solution)/shard_map/ppermute | solution.py:42
  688.1 81.0 %collective-permute-start.80 = (bf16[256,512]{1,0:T(8,128)(2,1)S(1)}, bf16[256,512]{1,0:T(8,128)(2,1)S(1)}, u32[]{:S(2)}, u32[]{:S(2)}) collective-permute-start(bf16[256,512]{1,0:T(8,128)(2,1)S(1)} %add_convert_fusion.1), channel_id=1, source_target_pairs={{18,0},{19,1},{16,2},{17,3},{22,4},{23,5},{20,6},{21,7},{26,8},{27... | collective-permute-start | bytes 786440 | tf_op jit(solution)/shard_map/ppermute | solution.py:42
  689.4 81.1 %collective-permute-start.79 = (bf16[256,512]{1,0:T(8,128)(2,1)S(1)}, bf16[256,512]{1,0:T(8,128)(2,1)S(1)}, u32[]{:S(2)}, u32[]{:S(2)}) collective-permute-start(bf16[256,512]{1,0:T(8,128)(2,1)S(1)} %add_convert_fusion.1), channel_id=1, source_target_pairs={{17,0},{18,1},{19,2},{16,3},{21,4},{22,5},{23,6},{20,7},{25,8},{26... | collective-permute-start | bytes 786440 | tf_op jit(solution)/shard_map/ppermute | solution.py:42
  690.7 81.2 %collective-permute-start.78 = (bf16[256,512]{1,0:T(8,128)(2,1)S(1)}, bf16[256,512]{1,0:T(8,128)(2,1)S(1)}, u32[]{:S(2)}, u32[]{:S(2)}) collective-permute-start(bf16[256,512]{1,0:T(8,128)(2,1)S(1)} %add_convert_fusion.1), channel_id=1, source_target_pairs={{16,0},{17,1},{18,2},{19,3},{20,4},{21,5},{22,6},{23,7},{24,8},{25... | collective-permute-start | bytes 786440 | tf_op jit(solution)/shard_map/ppermute | solution.py:42
  (88 other events, 1814.4 us)
Sparse Core Ops, SparseCore 0:
  428.4 73.2 all-gather.2

commit v2 on v1

v2 whole, which is shorter than its diff:
```python
import jax
import jax.numpy as jnp
from jax import lax
from jax.experimental import pallas as pl
from jax.experimental.pallas import tpu as pltpu
from jax.sharding import PartitionSpec as P

BF = jnp.bfloat16
F32 = jnp.float32
SIDE = 4
AXES = ("section", "kfac")


def silu_slope(values):
    sigmoid = jax.nn.sigmoid(values)
    return sigmoid * (1.0 + values * (1.0 - sigmoid))


def slot_numbers(owner_row):
    blocks = owner_row.shape[0]
    earlier = jnp.arange(blocks)[None, :] < jnp.arange(blocks)[:, None]
    shared = owner_row[None, :] == owner_row[:, None]
    return jnp.sum(jnp.logical_and(earlier, shared).astype(jnp.int32), axis=1)


def shift(block, rows, cols):
    route = []
    for row in range(SIDE):
        for col in range(SIDE):
            source = (row + rows) % SIDE * SIDE + (col + cols) % SIDE
            route.append((source, row * SIDE + col))
    return lax.ppermute(block, "kfac", route)


def shift_core(block, sections, step, rows, cols):
    size = SIDE * SIDE
    route = []
    for section in sections:
        for row in range(SIDE):
            for col in range(SIDE):
                source = (row + rows) % SIDE * SIDE + (col + cols) % SIDE
                route.append((section * size + source, (section - step) * size + row * SIDE + col))
    return lax.ppermute(block, AXES, route)


def dot_nt(left, right):
    return lax.dot_general(left, right, (((1,), (1,)), ((), ())), preferred_element_type=F32)


def dot_nn(left, right):
    return lax.dot_general(left, right, (((1,), (0,)), ((), ())), preferred_element_type=F32)


def move(position, sources, out_shapes, moves):
    count = len(sources)

    def body(position_ref, *refs):
        sems = refs[-1]
        pairs = moves(position_ref[0], position_ref[1], refs[:count], refs[count:-1])
        copies = [
            pltpu.make_async_copy(source, target, sems.at[i])
            for i, (source, target) in enumerate(pairs)
        ]
        for copy in copies:
            copy.start()
        for copy in copies:
            copy.wait()

    return pl.pallas_call(
        body,
        in_specs=[pl.BlockSpec(memory_space=pltpu.SMEM)] + [pl.BlockSpec(memory_space=pl.ANY)] * count,
        out_specs=[pl.BlockSpec(memory_space=pl.ANY)] * len(out_shapes),
        out_shape=out_shapes,
        scratch_shapes=[pltpu.SemaphoreType.DMA((SIDE * SIDE,))],
        cost_estimate=pl.CostEstimate(
            flops=0,
            bytes_accessed=2 * sum(o.size * o.dtype.itemsize for o in out_shapes),
            transcendentals=0,
        ),
    )(position, *sources)


def chunk(index, size):
    return pl.ds(pl.multiple_of(lax.rem(index + SIDE, SIDE) * size, size), size)


def whole(count):
    return [pl.BlockSpec(memory_space=pltpu.VMEM)] * count


def back_kernel(*refs):
    shards, weight_ref, out_ref = refs[:SIDE], refs[SIDE], refs[SIDE + 1]
    width = shards[0].shape[1]
    total = dot_nt(shards[0][...], weight_ref[:, :width])
    for j in range(1, SIDE):
        total = total + dot_nt(shards[j][...], weight_ref[:, j * width : (j + 1) * width])
    out_ref[...] = total.astype(out_ref.dtype)


def back_product(shards, weight):
    tokens, width = shards[0].shape
    block = weight.shape[0]
    return pl.pallas_call(
        back_kernel,
        in_specs=whole(SIDE + 1),
        out_specs=pl.BlockSpec(memory_space=pltpu.VMEM),
        out_shape=jax.ShapeDtypeStruct((tokens, block), BF),
        cost_estimate=pl.CostEstimate(
            flops=2 * tokens * width * SIDE * block,
            bytes_accessed=2 * SIDE * width * (tokens + block) + 2 * tokens * block,
            transcendentals=0,
        ),
    )(*shards, weight)


def proj_kernel(*refs):
    parts, factor_ref, weight_ref = refs[:SIDE], refs[SIDE], refs[SIDE + 1]
    slope_ref, own_ref, sent = refs[SIDE + 2], refs[SIDE + 3], refs[SIDE + 4 :]
    back = parts[0][...].astype(F32)
    for j in range(1, SIDE):
        back = back + parts[j][...].astype(F32)
    slope = (back * factor_ref[...]).astype(BF)
    slope_ref[...] = slope
    width = own_ref.shape[1]
    for j in range(1, SIDE):
        product = dot_nt(slope, weight_ref[j * width : (j + 1) * width, :])
        sent[j - 1][...] = product.astype(BF)
    own_ref[...] = dot_nt(slope, weight_ref[:width, :])


def proj_product(parts, factor, weight):
    tokens, block = factor.shape
    width = weight.shape[0] // SIDE
    bf = jax.ShapeDtypeStruct((tokens, width), BF)
    return pl.pallas_call(
        proj_kernel,
        in_specs=whole(SIDE + 2),
        out_specs=whole(SIDE + 1),
        out_shape=[
            jax.ShapeDtypeStruct((tokens, block), BF),
            jax.ShapeDtypeStruct((tokens, width), F32),
        ]
        + [bf] * (SIDE - 1),
        cost_estimate=pl.CostEstimate(
            flops=2 * tokens * width * SIDE * block,
            bytes_accessed=2 * SIDE * width * (tokens + block) + 12 * tokens * block,
            transcendentals=0,
        ),
    )(*parts, factor, weight)


def left_kernel(block_ref, factor_ref, x_ref, out_ref):
    out_ref[...] = dot_nt(factor_ref[...], x_ref[...]).astype(out_ref.dtype)


def left_product(block_here, factor, x):
    size = factor.shape[0]
    tokens = x.shape[0]
    return pl.pallas_call(
        left_kernel,
        grid_spec=pltpu.PrefetchScalarGridSpec(
            num_scalar_prefetch=1,
            grid=(1,),
            in_specs=[
                pl.BlockSpec((size, size), lambda i, block: (0, 0)),
                pl.BlockSpec((tokens, size), lambda i, block: (0, block[0])),
            ],
            out_specs=pl.BlockSpec((size, tokens), lambda i, block: (0, 0)),
        ),
        out_shape=jax.ShapeDtypeStruct((size, tokens), BF),
        cost_estimate=pl.CostEstimate(
            flops=2 * size * size * tokens,
            bytes_accessed=2 * size * (size + 2 * tokens),
            transcendentals=0,
        ),
    )(block_here, factor, x)


def spread_kernel(slots_ref, left_ref, right_ref, out_ref):
    out_ref[...] = dot_nn(left_ref[...], right_ref[...]).astype(out_ref.dtype)


def spread(slots, left, right, height):
    depth = left.shape[1]
    width = right.shape[1]
    block_count = slots.shape[0]
    return pl.pallas_call(
        spread_kernel,
        grid_spec=pltpu.PrefetchScalarGridSpec(
            num_scalar_prefetch=1,
            grid=(block_count,),
            in_specs=[
                pl.BlockSpec((height, depth), lambda b, slots: (slots[b], 0)),
                pl.BlockSpec((depth, width), lambda b, slots: (0, 0)),
            ],
            out_specs=pl.BlockSpec((height, width), lambda b, slots: (b, 0)),
        ),
        out_shape=jax.ShapeDtypeStruct((block_count * height, width), BF),
        cost_estimate=pl.CostEstimate(
            flops=2 * block_count * height * depth * width,
            bytes_accessed=2 * block_count * height * (depth + width),
            transcendentals=0,
        ),
    )(slots, left, right)


def on_device(
    top_cotangent, inputs, proj_weight, return_weight, owners, input_inverses, output_inverses
):
    section_count = lax.axis_size("section")
    section_here = lax.axis_index("section")
    kfac_here = lax.axis_index("kfac")
    row, col = kfac_here // SIDE, kfac_here % SIDE
    micro, per_micro, shard_width = top_cotangent.shape
    tokens = micro * per_micro
    x = inputs[0].reshape(tokens, -1)
    weight = proj_weight[0]
    returning = return_weight[0]
    width, stripe = weight.shape
    quarter = width // SIDE
    block_width = input_inverses.shape[2]
    block_count = width // block_width
    group_count = output_inverses.shape[1]

    position = jnp.stack([row, col]).astype(jnp.int32)
    block = SIDE * stripe
    back_cut = move(
        position,
        [returning],
        [jax.ShapeDtypeStruct((stripe, quarter), BF)] * SIDE,
        lambda r, c, ins, outs: [
            (ins[0].at[:, chunk(r - j, quarter)], outs[j]) for j in range(SIDE)
        ],
    )
    proj_cut = move(
        position,
        [weight],
        [jax.ShapeDtypeStruct((quarter, stripe), BF)] * SIDE,
        lambda r, c, ins, outs: [
            (ins[0].at[chunk(r - j, quarter), :], outs[j]) for j in range(SIDE)
        ],
    )
    back_parts = [back_cut[0]] + [shift(back_cut[j], j, 0) for j in range(1, SIDE)]
    top = top_cotangent.reshape(tokens, shard_width)
    first = list(range(section_count - 1, 0, -2))
    second = list(range(section_count - 2, -1, -2))
    incoming = [top] + [shift_core(top, first, 0, 0, j) for j in range(1, SIDE)]
    slopes_here = silu_slope(dot_nn(x, weight))
    slope_parts = [slopes_here] + [shift(slopes_here, j, 0) for j in range(1, SIDE)]
    proj_parts = [proj_cut[0]] + [shift(proj_cut[j], j, 0) for j in range(1, SIDE)]
    (back_weight,) = move(
        position,
        back_parts,
        [jax.ShapeDtypeStruct((block, quarter), BF)],
        lambda r, c, ins, outs: [
            (
                ins[j].at[:, chunk(c + k, shard_width)],
                outs[0].at[chunk(r + j, stripe), pl.ds(k * shard_width, shard_width)],
            )
            for j in range(SIDE)
            for k in range(SIDE)
        ],
    )
    (proj_block,) = move(
        position,
        proj_parts,
        [jax.ShapeDtypeStruct((quarter, block), BF)],
        lambda r, c, ins, outs: [
            (
                ins[j].at[chunk(c - k, shard_width), :],
                outs[0].at[pl.ds(k * shard_width, shard_width), chunk(r + j, stripe)],
            )
            for j in range(SIDE)
            for k in range(SIDE)
        ],
    )
    (factor,) = move(
        position,
        slope_parts,
        [jax.ShapeDtypeStruct((tokens, block), F32)],
        lambda r, c, ins, outs: [
            (ins[j], outs[0].at[:, chunk(r + j, stripe)]) for j in range(SIDE)
        ],
    )

    targets = owners[0] + slot_numbers(owners[0])
    mine = targets == kfac_here
    block_here = jnp.sum(jnp.where(mine, jnp.arange(block_count, dtype=jnp.int32), 0))
    left_here = left_product(block_here[None], input_inverses[0, 0], x)
    left_all = lax.all_gather(left_here, "kfac", axis=0, tiled=True)

    group_here = kfac_here * stripe // block_width
    per_group = SIDE // group_count
    out_cols = lax.dynamic_slice(
        output_inverses[0],
        (group_here, 0, kfac_here * stripe % block_width),
        (1, block_width, stripe),
    ).reshape(per_group, SIDE, stripe, stripe)
    out_rel = [
        lax.dynamic_index_in_dim(out_cols, (col + cols) % SIDE, 1, keepdims=False).reshape(
            per_group * stripe, stripe
        )
        for cols in range(SIDE)
    ]

    outputs = jnp.zeros((tokens, shard_width), BF)
    slope_saved = jnp.zeros((tokens, per_group * stripe), BF)
    for section in range(section_count - 1, -1, -1):
        active = section_here == section
        here = first if section in first else second
        back = back_product(incoming, back_weight)
        parts = [back] + [shift_core(back, here, 0, j, 0) for j in range(1, SIDE)]
        slope, own, *sent = proj_product(parts, factor, proj_block)
        slope_group = lax.dynamic_slice(
            slope, (0, group_here * per_group * stripe), (tokens, per_group * stripe)
        )
        slope_saved = jnp.where(active, slope_group, slope_saved)
        summed = incoming[0].astype(F32) + own
        for j in range(1, SIDE):
            summed = summed + shift_core(sent[j - 1], here, 0, 0, j).astype(F32)
        updated = summed.astype(BF)
        outputs = jnp.where(active, updated, outputs)
        if section > 0:
            senders = [s for s in here if s > 0]
            incoming = [shift_core(updated, senders, 1, 0, j) for j in range(SIDE)]

    right = dot_nn(slope_saved, out_rel[0])
    for cols in range(1, SIDE):
        right = right + dot_nn(shift(slope_saved, 0, cols), out_rel[cols])
    result = spread(targets, left_all, right.astype(BF), block_width)
    return outputs.reshape(1, micro, per_micro, shard_width), result[None]


def solution(mesh):
    return jax.shard_map(
        on_device,
        mesh=mesh,
        in_specs=(
            P(None, None, "kfac"),
            P("section", None, None, None),
            P("section", None, "kfac"),
            P("section", "kfac", None),
            P("section", None),
            P("section", "kfac", None, None),
            P("section", None, None, None),
        ),
        out_specs=(P("section", None, None, "kfac"), P("section", None, "kfac")),
        check_vma=False,
    )
```

time: 850 us -> 775 us (0.912)
  starting transfers between devices: 581 us -> 141 us
  Pallas kernels: 4.87 us -> 348 us
  waiting for transfers between devices: 98.9 us -> 231 us
  matrix products: 101 us -> 4.74 us
  local copies, waits for them, and re-layouts: 34.6 us -> 18.2 us
    ppermute x76 -> x79, starting transfers between devices: 544 us -> 123 us  [shift_core(): return lax.ppermute(block, AXES, route)]
    pallas_call x0 -> x22, Pallas kernels: none -> 340 us  [the longest x5 280 us: move(): pl.pallas_call(body, in_specs=[pl.BlockSpec(memory_space=pltpu.SMEM)] + [...]
    ppermute x76 -> x79, waiting for transfers between devices: 84.5 us -> 222 us  [shift_core(): return lax.ppermute(block, AXES, route)]
    dot_general x65 -> x0, matrix products: 94.8 us -> none  [dot_nt(): lax.dot_general(left, right, (((1,), (1,)), ((), ())), preferred_element_...]
    ppermute x15 -> x12, starting transfers between devices: 37.4 us -> 17.9 us  [shift(): return lax.ppermute(block, 'kfac', route)]
    unnamed x40 -> x150, local copies, waits for them, and re-layouts: 3.47 us -> 17.2 us
    all_gather x1 -> x0, local copies, waits for them, and re-layouts: 11.9 us -> none  [on_device(): left_all = lax.all_gather(left_here, 'kfac', axis=0)]
    dynamic_update_slice x11 -> x0, local copies, waits for them, and re-layouts: 10.1 us -> none  [the longest x4 5.42 us: on_device(): lax.dynamic_update_slice(back_weight, back_parts[rows], (place[rows], 0))]
  transfers between devices with their start and end apart: 92 -> 92, of which waited for: 7 -> 37; matrix products, arithmetic and copies ran while one was open for 12% -> 2% of each run, Pallas kernels for 0% -> 44%
where the time goes in v2:
time: 775 us; the launch traced here: 772 us
  Pallas kernels  348 us (45%)
  waiting for transfers between devices  231 us (30%)
  starting transfers between devices  141 us (18%)
  local copies, waits for them, and re-layouts  18.2 us (2%)
  between operations  15.7 us (2%)
  other arithmetic  14.4 us (2%)
    pallas_call x5, Pallas kernels, move(): pl.pallas_call(body, in_specs=[pl.BlockSpec(memory_space=pltpu.SMEM)] + [...  280 us
    ppermute x79, waiting for transfers between devices, shift_core(): return lax.ppermute(block, AXES, route)  222 us
    ppermute x79, starting transfers between devices, shift_core(): return lax.ppermute(block, AXES, route)  123 us
    pallas_call x8, Pallas kernels, proj_product(): pl.pallas_call(proj_kernel, in_specs=whole(SIDE + 2), out_specs=whole(SID...  29.9 us
    pallas_call x8, Pallas kernels, back_product(): pl.pallas_call(back_kernel, in_specs=whole(SIDE + 1), out_specs=pl.BlockS...  27 us
    ppermute x12, starting transfers between devices, shift(): return lax.ppermute(block, 'kfac', route)  17.9 us
    unnamed x150, local copies, waits for them, and re-layouts  17.2 us
  transfers between devices with their start and end apart: 92, of which 37 were waited for; matrix products, arithmetic and copies ran while one was open for 2% of the time, Pallas kernels for 44%

profile of v2, /device:TPU:0, one launch (start us, length us, event | category | flops | bytes accessed | tf_op | source)
XLA Modules:
  0.0 772.5 jit_solution(3685824659208013342)
XLA Ops:
  10.0 3.9 shard_map.107
  15.4 65.4 %shard_map.86 = (bf16[128,2048]{1,0:T(8,128)(2,1)}, bf16[128,2048]{1,0:T(8,128)(2,1)}, bf16[128,2048]{1,0:T(8,128)(2,1)}, bf16[128,2048]{1,0:T(8,128)(2,1)}) custom-call(s32[2]{0:T(128)} %pad_add_fusion.position_ref, bf16[128,8192]{1,0:T(8,128)(2,1)} %bitcast.34), custom_call_target="tpu_custom_call" | custom-call | bytes 4194304 | tf_op jit(solution)/shard_map/pallas_call | solution.py:69
  89.3 8.2 %collective-permute-done.9.refs_1_ = f32[256,128]{1,0:T(8,128)S(1)} collective-permute-done((f32[256,128]{1,0:T(8,128)S(1)}, f32[256,128]{1,0:T(8,128)S(1)}, u32[]{:S(2)}, u32[]{:S(2)}) %collective-permute-start.9) | collective-permute-done | bytes 131104 | tf_op jit(solution)/shard_map/ppermute | solution.py:32
  99.6 65.4 %shard_map.90 = (bf16[2048,128]{1,0:T(8,128)(2,1)}, bf16[2048,128]{1,0:T(8,128)(2,1)}, bf16[2048,128]{1,0:T(8,128)(2,1)}, bf16[2048,128]{1,0:T(8,128)(2,1)}) custom-call(s32[2]{0:T(128)} %pad_add_fusion.position_ref, bf16[8192,128]{1,0:T(8,128)(2,1)} %bitcast.35), custom_call_target="tpu_custom_call" | custom-call | bytes 4194304 | tf_op jit(solution)/shard_map/pallas_call | solution.py:69
  172.5 65.4 %shard_map.87.refs_4_ = bf16[512,2048]{1,0:T(8,128)(2,1)} custom-call(s32[2]{0:T(128)} %pad_add_fusion.position_ref, bf16[128,2048]{1,0:T(8,128)(2,1)} %get-tuple-element.50.refs_0_, bf16[128,2048]{1,0:T(8,128)(2,1)} %collective-permute-done.3.refs_1_, bf16[128,2048]{1,0:T(8,128)(2,1)} %copy-done.20, bf16[128,2048]{1,0:T(8,128)(2,1)} %copy-done.21), custom_call_target="tpu_custom_call" | custom-call | bytes 4194304 | tf_op jit(solution)/shard_map/pallas_call | solution.py:69
  243.4 17.8 %shard_map.89.refs_4_ = f32[256,512]{1,0:T(8,128)} custom-call(s32[2]{0:T(128)} %pad_add_fusion.position_ref, f32[256,128]{1,0:T(8,128)} %copy-done.71, f32[256,128]{1,0:T(8,128)} %copy-done.72, f32[256,128]{1,0:T(8,128)} %collective-permute-done.10.refs_2_, f32[256,128]{1,0:T(8,128)} %collective-permute-done.11.refs_3_), custom_call_target="tpu_custom_call" | custom-call | bytes 1048576 | tf_op jit(solution)/shard_map/pallas_call | solution.py:69
  262.3 65.4 %shard_map.91.refs_5_ = bf16[2048,512]{1,0:T(8,128)(2,1)} custom-call(s32[2]{0:T(128)} %pad_add_fusion.position_ref, bf16[2048,128]{1,0:T(8,128)(2,1)} %get-tuple-element.54.refs_0_, bf16[2048,128]{1,0:T(8,128)(2,1)} %copy-done.17, bf16[2048,128]{1,0:T(8,128)(2,1)} %copy-done.18, bf16[2048,128]{1,0:T(8,128)(2,1)} %copy-done.19), custom_call_target="tpu_custom_call" | custom-call | bytes 4194304 | tf_op jit(solution)/shard_map/pallas_call | solution.py:69
  341.5 29.8 %collective-permute-done.18.refs_0_ = bf16[256,512]{1,0:T(8,128)(2,1)S(1)} collective-permute-done((bf16[256,512]{1,0:T(8,128)(2,1)S(1)}, bf16[256,512]{1,0:T(8,128)(2,1)S(1)}, u32[]{:S(2)}, u32[]{:S(2)}) %collective-permute-start.18) | collective-permute-done | bytes 262176 | tf_op jit(solution)/shard_map/ppermute | solution.py:43
  371.2 6.0 collective-permute-done.19.refs_1_
  386.1 4.9 collective-permute-start.22
  396.1 5.0 collective-permute-done.23.refs_2_
  411.0 4.0 collective-permute-start.26
  448.6 33.5 %collective-permute-done.38.refs_0_ = bf16[256,512]{1,0:T(8,128)(2,1)S(1)} collective-permute-done((bf16[256,512]{1,0:T(8,128)(2,1)S(1)}, bf16[256,512]{1,0:T(8,128)(2,1)S(1)}, u32[]{:S(2)}, u32[]{:S(2)}) %collective-permute-start.38) | collective-permute-done | bytes 262176 | tf_op jit(solution)/shard_map/ppermute | solution.py:43
  482.1 4.7 collective-permute-done.39.refs_1_
  504.2 5.0 collective-permute-done.43.refs_2_
  519.1 4.0 collective-permute-start.46
  556.5 34.4 %collective-permute-done.58.refs_0_ = bf16[256,512]{1,0:T(8,128)(2,1)S(1)} collective-permute-done((bf16[256,512]{1,0:T(8,128)(2,1)S(1)}, bf16[256,512]{1,0:T(8,128)(2,1)S(1)}, u32[]{:S(2)}, u32[]{:S(2)}) %collective-permute-start.58) | collective-permute-done | bytes 262176 | tf_op jit(solution)/shard_map/ppermute | solution.py:43
  590.9 4.3 collective-permute-done.59.refs_1_
  612.6 4.7 collective-permute-done.63.refs_2_
  627.5 4.0 collective-permute-start.66
  664.9 35.8 %collective-permute-done.78.refs_0_ = bf16[256,512]{1,0:T(8,128)(2,1)S(1)} collective-permute-done((bf16[256,512]{1,0:T(8,128)(2,1)S(1)}, bf16[256,512]{1,0:T(8,128)(2,1)S(1)}, u32[]{:S(2)}, u32[]{:S(2)}) %collective-permute-start.78) | collective-permute-done | bytes 262176 | tf_op jit(solution)/shard_map/ppermute | solution.py:43
  700.7 4.3 collective-permute-done.79.refs_1_
  722.4 4.6 collective-permute-done.83.refs_2_
  757.9 7.8 %shard_map.108 = bf16[8192,128]{1,0:T(8,128)(2,1)} custom-call(s32[8]{0:T(128)} %get-tuple-element.99.slots_ref, bf16[16384,256]{1,0:T(8,128)(2,1)} %all-gather.2.cloned.1.call-done.left_ref, bf16[256,128]{1,0:T(8,128)(2,1)} %fusion.1.right_ref), custom_call_target="tpu_custom_call" | custom-call | flops 536870912 | bytes 6291456 | tf_op jit(solution)/shard_map/pallas_call | solution.py:187
  (353 shorter events, 268.4 us)
Async XLA Ops:
  7.2 750.7 %all-gather.2.cloned.1.call-start = ((), (), s32[]{:S(2)}) async-start(), calls=%async_computation | async-start | bytes 8912896 | tf_op jit(solution)/shard_map/all_gather | solution.py:290
  14.0 84.9 %collective-permute-start = (bf16[256,512]{1,0:T(8,128)(2,1)S(1)}, bf16[256,512]{1,0:T(8,128)(2,1)S(1)}, u32[]{:S(2)}, u32[]{:S(2)}) collective-permute-start(bf16[256,512]{1,0:T(8,128)(2,1)S(1)} %bitcast.40), channel_id=1, source_target_pairs={{113,112},{114,113},{115,114},{112,115},{117,116},{118,117},{119,1... | collective-permute-start | bytes 786440 | tf_op jit(solution)/shard_map/ppermute | solution.py:43
  80.8 87.6 %collective-permute-start.3 = (bf16[128,2048]{1,0:T(8,128)(2,1)}, bf16[128,2048]{1,0:T(8,128)(2,1)}, u32[]{:S(2)}, u32[]{:S(2)}) collective-permute-start(bf16[128,2048]{1,0:T(8,128)(2,1)} %get-tuple-element.51), channel_id=1, source_target_pairs={{4,0},{5,1},{6,2},{7,3},{8,4},{9,5},{10,6},{11,7},{12,8},{13,9},{1... | collective-permute-start | bytes 1572872 | tf_op jit(solution)/shard_map/ppermute | solution.py:32
  88.3 76.8 %collective-permute-start.1 = (bf16[256,512]{1,0:T(8,128)(2,1)S(1)}, bf16[256,512]{1,0:T(8,128)(2,1)S(1)}, u32[]{:S(2)}, u32[]{:S(2)}) collective-permute-start(bf16[256,512]{1,0:T(8,128)(2,1)S(1)} %bitcast.41), channel_id=1, source_target_pairs={{114,112},{115,113},{112,114},{113,115},{118,116},{119,117},{116,1... | collective-permute-start | bytes 786440 | tf_op jit(solution)/shard_map/ppermute | solution.py:43
  88.9 80.8 %collective-permute-start.4 = (bf16[128,2048]{1,0:T(8,128)(2,1)}, bf16[128,2048]{1,0:T(8,128)(2,1)S(1)}, u32[]{:S(2)}, u32[]{:S(2)}) collective-permute-start(bf16[128,2048]{1,0:T(8,128)(2,1)} %get-tuple-element.52), channel_id=1, source_target_pairs={{8,0},{9,1},{10,2},{11,3},{12,4},{13,5},{14,6},{15,7},{0,8},{1,9},... | collective-permute-start | bytes 1572872 | tf_op jit(solution)/shard_map/ppermute | solution.py:32
  97.5 73.9 %collective-permute-start.5 = (bf16[128,2048]{1,0:T(8,128)(2,1)}, bf16[128,2048]{1,0:T(8,128)(2,1)S(1)}, u32[]{:S(2)}, u32[]{:S(2)}) collective-permute-start(bf16[128,2048]{1,0:T(8,128)(2,1)} %get-tuple-element.53), channel_id=1, source_target_pairs={{12,0},{13,1},{14,2},{15,3},{0,4},{1,5},{2,6},{3,7},{4,8},{5,9},{6... | collective-permute-start | bytes 1572872 | tf_op jit(solution)/shard_map/ppermute | solution.py:32
  98.9 68.1 %collective-permute-start.2 = (bf16[256,512]{1,0:T(8,128)(2,1)S(1)}, bf16[256,512]{1,0:T(8,128)(2,1)S(1)}, u32[]{:S(2)}, u32[]{:S(2)}) collective-permute-start(bf16[256,512]{1,0:T(8,128)(2,1)S(1)} %bitcast.42), channel_id=1, source_target_pairs={{115,112},{112,113},{113,114},{114,115},{119,116},{116,117},{117,1... | collective-permute-start | bytes 786440 | tf_op jit(solution)/shard_map/ppermute | solution.py:43
  165.0 77.7 %collective-permute-start.12 = (bf16[2048,128]{1,0:T(8,128)(2,1)}, bf16[2048,128]{1,0:T(8,128)(2,1)S(1)}, u32[]{:S(2)}, u32[]{:S(2)}) collective-permute-start(bf16[2048,128]{1,0:T(8,128)(2,1)} %get-tuple-element.55), channel_id=1, source_target_pairs={{4,0},{5,1},{6,2},{7,3},{8,4},{9,5},{10,6},{11,7},{12,8},{13,9},{1... | collective-permute-start | bytes 1572872 | tf_op jit(solution)/shard_map/ppermute | solution.py:32
  166.9 94.3 %collective-permute-start.13 = (bf16[2048,128]{1,0:T(8,128)(2,1)}, bf16[2048,128]{1,0:T(8,128)(2,1)S(1)}, u32[]{:S(2)}, u32[]{:S(2)}) collective-permute-start(bf16[2048,128]{1,0:T(8,128)(2,1)} %get-tuple-element.56), channel_id=1, source_target_pairs={{8,0},{9,1},{10,2},{11,3},{12,4},{13,5},{14,6},{15,7},{0,8},{1,9},... | collective-permute-start | bytes 1572872 | tf_op jit(solution)/shard_map/ppermute | solution.py:32
  168.4 92.9 %collective-permute-start.14 = (bf16[2048,128]{1,0:T(8,128)(2,1)}, bf16[2048,128]{1,0:T(8,128)(2,1)S(1)}, u32[]{:S(2)}, u32[]{:S(2)}) collective-permute-start(bf16[2048,128]{1,0:T(8,128)(2,1)} %get-tuple-element.57), channel_id=1, source_target_pairs={{12,0},{13,1},{14,2},{15,3},{0,4},{1,5},{2,6},{3,7},{4,8},{5,9},{6... | collective-permute-start | bytes 1572872 | tf_op jit(solution)/shard_map/ppermute | solution.py:32
  169.8 71.6 %collective-permute-start.10 = (f32[256,128]{1,0:T(8,128)S(1)}, f32[256,128]{1,0:T(8,128)}, u32[]{:S(2)}, u32[]{:S(2)}) collective-permute-start(f32[256,128]{1,0:T(8,128)S(1)} %add_multiply_fusion.refs_0_), channel_id=1, source_target_pairs={{8,0},{9,1},{10,2},{11,3},{12,4},{13,5},{14,6},{15,7},{0,8},{1,9},... | collective-permute-start | bytes 393224 | tf_op jit(solution)/shard_map/ppermute | solution.py:32
  171.4 70.7 %collective-permute-start.11 = (f32[256,128]{1,0:T(8,128)S(1)}, f32[256,128]{1,0:T(8,128)}, u32[]{:S(2)}, u32[]{:S(2)}) collective-permute-start(f32[256,128]{1,0:T(8,128)S(1)} %add_multiply_fusion.refs_0_), channel_id=1, source_target_pairs={{12,0},{13,1},{14,2},{15,3},{0,4},{1,5},{2,6},{3,7},{4,8},{5,9},{6... | collective-permute-start | bytes 393224 | tf_op jit(solution)/shard_map/ppermute | solution.py:32
  241.4 86.4 %collective-permute-start.6 = (bf16[256,512]{1,0:T(8,128)(2,1)}, bf16[256,512]{1,0:T(8,128)(2,1)S(1)}, u32[]{:S(2)}, u32[]{:S(2)}) collective-permute-start(bf16[256,512]{1,0:T(8,128)(2,1)} %shard_map.88.refs_0_), channel_id=1, source_target_pairs={{116,112},{117,113},{118,114},{119,115},{120,116},{121,117},{122,1... | collective-permute-start | bytes 786440 | tf_op jit(solution)/shard_map/ppermute | solution.py:43
  242.0 85.7 %collective-permute-start.7 = (bf16[256,512]{1,0:T(8,128)(2,1)}, bf16[256,512]{1,0:T(8,128)(2,1)S(1)}, u32[]{:S(2)}, u32[]{:S(2)}) collective-permute-start(bf16[256,512]{1,0:T(8,128)(2,1)} %shard_map.88.refs_0_), channel_id=1, source_target_pairs={{120,112},{121,113},{122,114},{123,115},{124,116},{125,117},{126,1... | collective-permute-start | bytes 786440 | tf_op jit(solution)/shard_map/ppermute | solution.py:43
  242.7 85.0 %collective-permute-start.8 = (bf16[256,512]{1,0:T(8,128)(2,1)}, bf16[256,512]{1,0:T(8,128)(2,1)S(1)}, u32[]{:S(2)}, u32[]{:S(2)}) collective-permute-start(bf16[256,512]{1,0:T(8,128)(2,1)} %shard_map.88.refs_0_), channel_id=1, source_target_pairs={{124,112},{125,113},{126,114},{127,115},{112,116},{113,117},{114,1... | collective-permute-start | bytes 786440 | tf_op jit(solution)/shard_map/ppermute | solution.py:43
  444.7 42.1 %collective-permute-start.39 = (bf16[256,512]{1,0:T(8,128)(2,1)S(1)}, bf16[256,512]{1,0:T(8,128)(2,1)S(1)}, u32[]{:S(2)}, u32[]{:S(2)}) collective-permute-start(bf16[256,512]{1,0:T(8,128)(2,1)S(1)} %add_convert_fusion.5), channel_id=1, source_target_pairs={{113,96},{114,97},{115,98},{112,99},{117,100},{118,101},{119,102},... | collective-permute-start | bytes 786440 | tf_op jit(solution)/shard_map/ppermute | solution.py:43
  446.0 42.8 %collective-permute-start.40 = (bf16[256,512]{1,0:T(8,128)(2,1)S(1)}, bf16[256,512]{1,0:T(8,128)(2,1)S(1)}, u32[]{:S(2)}, u32[]{:S(2)}) collective-permute-start(bf16[256,512]{1,0:T(8,128)(2,1)S(1)} %add_convert_fusion.5), channel_id=1, source_target_pairs={{114,96},{115,97},{112,98},{113,99},{118,100},{119,101},{116,102},... | collective-permute-start | bytes 786440 | tf_op jit(solution)/shard_map/ppermute | solution.py:43
  447.3 44.2 %collective-permute-start.41 = (bf16[256,512]{1,0:T(8,128)(2,1)S(1)}, bf16[256,512]{1,0:T(8,128)(2,1)S(1)}, u32[]{:S(2)}, u32[]{:S(2)}) collective-permute-start(bf16[256,512]{1,0:T(8,128)(2,1)S(1)} %add_convert_fusion.5), channel_id=1, source_target_pairs={{115,96},{112,97},{113,98},{114,99},{119,100},{116,101},{117,102},... | collective-permute-start | bytes 786440 | tf_op jit(solution)/shard_map/ppermute | solution.py:43
  552.6 42.6 %collective-permute-start.59 = (bf16[256,512]{1,0:T(8,128)(2,1)S(1)}, bf16[256,512]{1,0:T(8,128)(2,1)S(1)}, u32[]{:S(2)}, u32[]{:S(2)}) collective-permute-start(bf16[256,512]{1,0:T(8,128)(2,1)S(1)} %add_convert_fusion.3), channel_id=1, source_target_pairs={{113,96},{114,97},{115,98},{112,99},{117,100},{118,101},{119,102},... | collective-permute-start | bytes 786440 | tf_op jit(solution)/shard_map/ppermute | solution.py:43
  553.9 43.3 %collective-permute-start.60 = (bf16[256,512]{1,0:T(8,128)(2,1)S(1)}, bf16[256,512]{1,0:T(8,128)(2,1)S(1)}, u32[]{:S(2)}, u32[]{:S(2)}) collective-permute-start(bf16[256,512]{1,0:T(8,128)(2,1)S(1)} %add_convert_fusion.3), channel_id=1, source_target_pairs={{114,96},{115,97},{112,98},{113,99},{118,100},{119,101},{116,102},... | collective-permute-start | bytes 786440 | tf_op jit(solution)/shard_map/ppermute | solution.py:43
  555.2 44.7 %collective-permute-start.61 = (bf16[256,512]{1,0:T(8,128)(2,1)S(1)}, bf16[256,512]{1,0:T(8,128)(2,1)S(1)}, u32[]{:S(2)}, u32[]{:S(2)}) collective-permute-start(bf16[256,512]{1,0:T(8,128)(2,1)S(1)} %add_convert_fusion.3), channel_id=1, source_target_pairs={{115,96},{112,97},{113,98},{114,99},{119,100},{116,101},{117,102},... | collective-permute-start | bytes 786440 | tf_op jit(solution)/shard_map/ppermute | solution.py:43
  661.0 44.0 %collective-permute-start.79 = (bf16[256,512]{1,0:T(8,128)(2,1)S(1)}, bf16[256,512]{1,0:T(8,128)(2,1)S(1)}, u32[]{:S(2)}, u32[]{:S(2)}) collective-permute-start(bf16[256,512]{1,0:T(8,128)(2,1)S(1)} %add_convert_fusion.1), channel_id=1, source_target_pairs={{113,96},{114,97},{115,98},{112,99},{117,100},{118,101},{119,102},... | collective-permute-start | bytes 786440 | tf_op jit(solution)/shard_map/ppermute | solution.py:43
  662.3 44.7 %collective-permute-start.80 = (bf16[256,512]{1,0:T(8,128)(2,1)S(1)}, bf16[256,512]{1,0:T(8,128)(2,1)S(1)}, u32[]{:S(2)}, u32[]{:S(2)}) collective-permute-start(bf16[256,512]{1,0:T(8,128)(2,1)S(1)} %add_convert_fusion.1), channel_id=1, source_target_pairs={{114,96},{115,97},{112,98},{113,99},{118,100},{119,101},{116,102},... | collective-permute-start | bytes 786440 | tf_op jit(solution)/shard_map/ppermute | solution.py:43
  663.6 46.1 %collective-permute-start.81 = (bf16[256,512]{1,0:T(8,128)(2,1)S(1)}, bf16[256,512]{1,0:T(8,128)(2,1)S(1)}, u32[]{:S(2)}, u32[]{:S(2)}) collective-permute-start(bf16[256,512]{1,0:T(8,128)(2,1)S(1)} %add_convert_fusion.1), channel_id=1, source_target_pairs={{115,96},{112,97},{113,98},{114,99},{119,100},{116,101},{117,102},... | collective-permute-start | bytes 786440 | tf_op jit(solution)/shard_map/ppermute | solution.py:43
  (143 other events, 1575.6 us)
Sparse Core Ops, SparseCore 0:
  14.1 73.0 all-gather.1

commit v3 on v2

--- a/solution.py
+++ b/solution.py
@@ -55,23 +55,14 @@
     count = len(sources)
 
     def body(position_ref, *refs):
-        sems = refs[-1]
-        pairs = moves(position_ref[0], position_ref[1], refs[:count], refs[count:-1])
-        copies = [
-            pltpu.make_async_copy(source, target, sems.at[i])
-            for i, (source, target) in enumerate(pairs)
-        ]
-        for copy in copies:
-            copy.start()
-        for copy in copies:
-            copy.wait()
+        for source, target in moves(position_ref[0], position_ref[1], refs[:count], refs[count:]):
+            target[...] = source[...]
 
     return pl.pallas_call(
         body,
-        in_specs=[pl.BlockSpec(memory_space=pltpu.SMEM)] + [pl.BlockSpec(memory_space=pl.ANY)] * count,
-        out_specs=[pl.BlockSpec(memory_space=pl.ANY)] * len(out_shapes),
+        in_specs=[pl.BlockSpec(memory_space=pltpu.SMEM)] + whole(count),
+        out_specs=whole(len(out_shapes)),
         out_shape=out_shapes,
-        scratch_shapes=[pltpu.SemaphoreType.DMA((SIDE * SIDE,))],
         cost_estimate=pl.CostEstimate(
             flops=0,
             bytes_accessed=2 * sum(o.size * o.dtype.itemsize for o in out_shapes),

time: 775 us -> 570 us (0.74)
  Pallas kernels: 348 us -> 83.5 us
  waiting for transfers between devices: 231 us -> 284 us
    pallas_call x5, Pallas kernels: 280 us -> 14.6 us  [move(): pl.pallas_call(body, in_specs=[pl.BlockSpec(memory_space=pltpu.SMEM)] + w...]
    ppermute x79, waiting for transfers between devices: 222 us -> 253 us  [shift_core(): return lax.ppermute(block, AXES, route)]
    ppermute x12, waiting for transfers between devices: 8.24 us -> 30.5 us  [shift(): return lax.ppermute(block, 'kfac', route)]
  transfers between devices with their start and end apart: 92 -> 92, of which waited for: 37 -> 40; matrix products, arithmetic and copies ran while one was open for 2% -> 3% of each run, Pallas kernels for 44% -> 13%
where the time goes in v3:
time: 570 us; the launch traced here: 567 us
  waiting for transfers between devices  284 us (50%)
  starting transfers between devices  147 us (26%)
  Pallas kernels  83.5 us (15%)
  local copies, waits for them, and re-layouts  18.2 us (3%)
  between operations  15.6 us (3%)
  other arithmetic  14.4 us (3%)
    ppermute x79, waiting for transfers between devices, shift_core(): return lax.ppermute(block, AXES, route)  253 us
    ppermute x79, starting transfers between devices, shift_core(): return lax.ppermute(block, AXES, route)  123 us
    ppermute x12, waiting for transfers between devices, shift(): return lax.ppermute(block, 'kfac', route)  30.5 us
    pallas_call x8, Pallas kernels, proj_product(): pl.pallas_call(proj_kernel, in_specs=whole(SIDE + 2), out_specs=whole(SID...  29.9 us
    pallas_call x8, Pallas kernels, back_product(): pl.pallas_call(back_kernel, in_specs=whole(SIDE + 1), out_specs=pl.BlockS...  27.3 us
    ppermute x12, starting transfers between devices, shift(): return lax.ppermute(block, 'kfac', route)  24.1 us
    unnamed x150, local copies, waits for them, and re-layouts  17.2 us
    pallas_call x5, Pallas kernels, move(): pl.pallas_call(body, in_specs=[pl.BlockSpec(memory_space=pltpu.SMEM)] + w...  14.6 us
  transfers between devices with their start and end apart: 92, of which 40 were waited for; matrix products, arithmetic and copies ran while one was open for 3% of the time, Pallas kernels for 13%

profile of v3, /device:TPU:0, one launch (start us, length us, event | category | flops | bytes accessed | tf_op | source)
XLA Modules:
  0.0 567.2 jit_solution(14846423198965203898)
XLA Ops:
  10.0 3.9 shard_map.107
  26.8 14.7 %collective-permute-done.9.refs_1_ = f32[256,128]{1,0:T(8,128)S(1)} collective-permute-done((f32[256,128]{1,0:T(8,128)S(1)}, f32[256,128]{1,0:T(8,128)S(1)}, u32[]{:S(2)}, u32[]{:S(2)}) %collective-permute-start.9) | collective-permute-done | bytes 131104 | tf_op jit(solution)/shard_map/ppermute | solution.py:32
  45.3 4.4 collective-permute-start.12
  56.4 7.0 %collective-permute-start.11 = (f32[256,128]{1,0:T(8,128)S(1)}, f32[256,128]{1,0:T(8,128)}, u32[]{:S(2)}, u32[]{:S(2)}) collective-permute-start(f32[256,128]{1,0:T(8,128)S(1)} %add_multiply_fusion.refs_0_), channel_id=1, source_target_pairs={{12,0},{13,1},{14,2},{15,3},{0,4},{1,5},{2,6},{3,7},{4,8},{5,9},{6... | collective-permute-start | bytes 393224 | tf_op jit(solution)/shard_map/ppermute | solution.py:32
  70.1 8.1 %collective-permute-done.10.refs_2_ = f32[256,128]{1,0:T(8,128)} collective-permute-done((f32[256,128]{1,0:T(8,128)S(1)}, f32[256,128]{1,0:T(8,128)}, u32[]{:S(2)}, u32[]{:S(2)}) %collective-permute-start.10) | collective-permute-done | bytes 131104 | tf_op jit(solution)/shard_map/ppermute | solution.py:32
  78.9 4.7 collective-permute-done.11.refs_3_
  105.2 62.2 %collective-permute-done.18.refs_0_ = bf16[256,512]{1,0:T(8,128)(2,1)S(1)} collective-permute-done((bf16[256,512]{1,0:T(8,128)(2,1)S(1)}, bf16[256,512]{1,0:T(8,128)(2,1)S(1)}, u32[]{:S(2)}, u32[]{:S(2)}) %collective-permute-start.18) | collective-permute-done | bytes 262176 | tf_op jit(solution)/shard_map/ppermute | solution.py:43
  167.4 4.7 collective-permute-done.19.refs_1_
  189.5 4.7 collective-permute-done.23.refs_2_
  204.2 4.0 collective-permute-start.26
  241.8 34.8 %collective-permute-done.38.refs_0_ = bf16[256,512]{1,0:T(8,128)(2,1)S(1)} collective-permute-done((bf16[256,512]{1,0:T(8,128)(2,1)S(1)}, bf16[256,512]{1,0:T(8,128)(2,1)S(1)}, u32[]{:S(2)}, u32[]{:S(2)}) %collective-permute-start.38) | collective-permute-done | bytes 262176 | tf_op jit(solution)/shard_map/ppermute | solution.py:43
  276.6 4.3 collective-permute-done.39.refs_1_
  298.3 4.5 collective-permute-done.43.refs_2_
  312.9 4.0 collective-permute-start.46
  316.9 3.9 collective-permute-start.45
  350.3 35.4 %collective-permute-done.58.refs_0_ = bf16[256,512]{1,0:T(8,128)(2,1)S(1)} collective-permute-done((bf16[256,512]{1,0:T(8,128)(2,1)S(1)}, bf16[256,512]{1,0:T(8,128)(2,1)S(1)}, u32[]{:S(2)}, u32[]{:S(2)}) %collective-permute-start.58) | collective-permute-done | bytes 262176 | tf_op jit(solution)/shard_map/ppermute | solution.py:43
  385.7 4.1 collective-permute-done.59.refs_1_
  407.3 4.2 collective-permute-done.63.refs_2_
  421.8 4.0 collective-permute-start.66
  425.8 3.9 collective-permute-start.65
  459.4 36.5 %collective-permute-done.78.refs_0_ = bf16[256,512]{1,0:T(8,128)(2,1)S(1)} collective-permute-done((bf16[256,512]{1,0:T(8,128)(2,1)S(1)}, bf16[256,512]{1,0:T(8,128)(2,1)S(1)}, u32[]{:S(2)}, u32[]{:S(2)}) %collective-permute-start.78) | collective-permute-done | bytes 262176 | tf_op jit(solution)/shard_map/ppermute | solution.py:43
  496.0 4.3 collective-permute-done.79.refs_1_
  517.7 4.0 collective-permute-done.83.refs_2_
  552.6 7.8 %shard_map.108 = bf16[8192,128]{1,0:T(8,128)(2,1)} custom-call(s32[8]{0:T(128)} %get-tuple-element.99.slots_ref, bf16[16384,256]{1,0:T(8,128)(2,1)} %all-gather.2.cloned.1.call-done.left_ref, bf16[256,128]{1,0:T(8,128)(2,1)} %fusion.1.right_ref), custom_call_target="tpu_custom_call" | custom-call | flops 536870912 | bytes 6291456 | tf_op jit(solution)/shard_map/pallas_call | solution.py:178
  (353 shorter events, 277.5 us)
Async XLA Ops:
  7.2 545.4 %all-gather.2.cloned.1.call-start = ((), (), s32[]{:S(2)}) async-start(), calls=%async_computation | async-start | bytes 8912896 | tf_op jit(solution)/shard_map/all_gather | solution.py:281
  14.0 27.6 %collective-permute-start = (bf16[256,512]{1,0:T(8,128)(2,1)S(1)}, bf16[256,512]{1,0:T(8,128)(2,1)S(1)}, u32[]{:S(2)}, u32[]{:S(2)}) collective-permute-start(bf16[256,512]{1,0:T(8,128)(2,1)S(1)} %bitcast.40), channel_id=1, source_target_pairs={{113,112},{114,113},{115,114},{112,115},{117,116},{118,117},{119,1... | collective-permute-start | bytes 786440 | tf_op jit(solution)/shard_map/ppermute | solution.py:43
  18.4 32.9 %collective-permute-start.3 = (bf16[128,2048]{1,0:T(8,128)(2,1)}, bf16[128,2048]{1,0:T(8,128)(2,1)}, u32[]{:S(2)}, u32[]{:S(2)}) collective-permute-start(bf16[128,2048]{1,0:T(8,128)(2,1)} %get-tuple-element.51), channel_id=1, source_target_pairs={{4,0},{5,1},{6,2},{7,3},{8,4},{9,5},{10,6},{11,7},{12,8},{13,9},{1... | collective-permute-start | bytes 1572872 | tf_op jit(solution)/shard_map/ppermute | solution.py:32
  26.5 26.2 %collective-permute-start.4 = (bf16[128,2048]{1,0:T(8,128)(2,1)}, bf16[128,2048]{1,0:T(8,128)(2,1)S(1)}, u32[]{:S(2)}, u32[]{:S(2)}) collective-permute-start(bf16[128,2048]{1,0:T(8,128)(2,1)} %get-tuple-element.52), channel_id=1, source_target_pairs={{8,0},{9,1},{10,2},{11,3},{12,4},{13,5},{14,6},{15,7},{0,8},{1,9},... | collective-permute-start | bytes 1572872 | tf_op jit(solution)/shard_map/ppermute | solution.py:32
  45.3 39.0 %collective-permute-start.12 = (bf16[2048,128]{1,0:T(8,128)(2,1)}, bf16[2048,128]{1,0:T(8,128)(2,1)S(1)}, u32[]{:S(2)}, u32[]{:S(2)}) collective-permute-start(bf16[2048,128]{1,0:T(8,128)(2,1)} %get-tuple-element.55), channel_id=1, source_target_pairs={{4,0},{5,1},{6,2},{7,3},{8,4},{9,5},{10,6},{11,7},{12,8},{13,9},{1... | collective-permute-start | bytes 1572872 | tf_op jit(solution)/shard_map/ppermute | solution.py:32
  49.8 37.2 %collective-permute-start.13 = (bf16[2048,128]{1,0:T(8,128)(2,1)}, bf16[2048,128]{1,0:T(8,128)(2,1)S(1)}, u32[]{:S(2)}, u32[]{:S(2)}) collective-permute-start(bf16[2048,128]{1,0:T(8,128)(2,1)} %get-tuple-element.56), channel_id=1, source_target_pairs={{8,0},{9,1},{10,2},{11,3},{12,4},{13,5},{14,6},{15,7},{0,8},{1,9},... | collective-permute-start | bytes 1572872 | tf_op jit(solution)/shard_map/ppermute | solution.py:32
  51.3 35.7 %collective-permute-start.14 = (bf16[2048,128]{1,0:T(8,128)(2,1)}, bf16[2048,128]{1,0:T(8,128)(2,1)S(1)}, u32[]{:S(2)}, u32[]{:S(2)}) collective-permute-start(bf16[2048,128]{1,0:T(8,128)(2,1)} %get-tuple-element.57), channel_id=1, source_target_pairs={{12,0},{13,1},{14,2},{15,3},{0,4},{1,5},{2,6},{3,7},{4,8},{5,9},{6... | collective-permute-start | bytes 1572872 | tf_op jit(solution)/shard_map/ppermute | solution.py:32
  56.4 27.3 %collective-permute-start.11 = (f32[256,128]{1,0:T(8,128)S(1)}, f32[256,128]{1,0:T(8,128)}, u32[]{:S(2)}, u32[]{:S(2)}) collective-permute-start(f32[256,128]{1,0:T(8,128)S(1)} %add_multiply_fusion.refs_0_), channel_id=1, source_target_pairs={{12,0},{13,1},{14,2},{15,3},{0,4},{1,5},{2,6},{3,7},{4,8},{5,9},{6... | collective-permute-start | bytes 393224 | tf_op jit(solution)/shard_map/ppermute | solution.py:32
  100.0 67.4 %collective-permute-start.18 = (bf16[256,512]{1,0:T(8,128)(2,1)S(1)}, bf16[256,512]{1,0:T(8,128)(2,1)S(1)}, u32[]{:S(2)}, u32[]{:S(2)}) collective-permute-start(bf16[256,512]{1,0:T(8,128)(2,1)S(1)} %add_convert_fusion.7), channel_id=1, source_target_pairs={{112,96},{113,97},{114,98},{115,99},{116,100},{117,101},{118,102},... | collective-permute-start | bytes 786440 | tf_op jit(solution)/shard_map/ppermute | solution.py:43
  101.3 70.8 %collective-permute-start.19 = (bf16[256,512]{1,0:T(8,128)(2,1)S(1)}, bf16[256,512]{1,0:T(8,128)(2,1)S(1)}, u32[]{:S(2)}, u32[]{:S(2)}) collective-permute-start(bf16[256,512]{1,0:T(8,128)(2,1)S(1)} %add_convert_fusion.7), channel_id=1, source_target_pairs={{113,96},{114,97},{115,98},{112,99},{117,100},{118,101},{119,102},... | collective-permute-start | bytes 786440 | tf_op jit(solution)/shard_map/ppermute | solution.py:43
  102.6 71.5 %collective-permute-start.20 = (bf16[256,512]{1,0:T(8,128)(2,1)S(1)}, bf16[256,512]{1,0:T(8,128)(2,1)S(1)}, u32[]{:S(2)}, u32[]{:S(2)}) collective-permute-start(bf16[256,512]{1,0:T(8,128)(2,1)S(1)} %add_convert_fusion.7), channel_id=1, source_target_pairs={{114,96},{115,97},{112,98},{113,99},{118,100},{119,101},{116,102},... | collective-permute-start | bytes 786440 | tf_op jit(solution)/shard_map/ppermute | solution.py:43
  103.9 72.9 %collective-permute-start.21 = (bf16[256,512]{1,0:T(8,128)(2,1)S(1)}, bf16[256,512]{1,0:T(8,128)(2,1)S(1)}, u32[]{:S(2)}, u32[]{:S(2)}) collective-permute-start(bf16[256,512]{1,0:T(8,128)(2,1)S(1)} %add_convert_fusion.7), channel_id=1, source_target_pairs={{115,96},{112,97},{113,98},{114,99},{119,100},{116,101},{117,102},... | collective-permute-start | bytes 786440 | tf_op jit(solution)/shard_map/ppermute | solution.py:43
  236.6 40.0 %collective-permute-start.38 = (bf16[256,512]{1,0:T(8,128)(2,1)S(1)}, bf16[256,512]{1,0:T(8,128)(2,1)S(1)}, u32[]{:S(2)}, u32[]{:S(2)}) collective-permute-start(bf16[256,512]{1,0:T(8,128)(2,1)S(1)} %add_convert_fusion.5), channel_id=1, source_target_pairs={{112,96},{113,97},{114,98},{115,99},{116,100},{117,101},{118,102},... | collective-permute-start | bytes 786440 | tf_op jit(solution)/shard_map/ppermute | solution.py:43
  237.9 43.0 %collective-permute-start.39 = (bf16[256,512]{1,0:T(8,128)(2,1)S(1)}, bf16[256,512]{1,0:T(8,128)(2,1)S(1)}, u32[]{:S(2)}, u32[]{:S(2)}) collective-permute-start(bf16[256,512]{1,0:T(8,128)(2,1)S(1)} %add_convert_fusion.5), channel_id=1, source_target_pairs={{113,96},{114,97},{115,98},{112,99},{117,100},{118,101},{119,102},... | collective-permute-start | bytes 786440 | tf_op jit(solution)/shard_map/ppermute | solution.py:43
  239.2 43.7 %collective-permute-start.40 = (bf16[256,512]{1,0:T(8,128)(2,1)S(1)}, bf16[256,512]{1,0:T(8,128)(2,1)S(1)}, u32[]{:S(2)}, u32[]{:S(2)}) collective-permute-start(bf16[256,512]{1,0:T(8,128)(2,1)S(1)} %add_convert_fusion.5), channel_id=1, source_target_pairs={{114,96},{115,97},{112,98},{113,99},{118,100},{119,101},{116,102},... | collective-permute-start | bytes 786440 | tf_op jit(solution)/shard_map/ppermute | solution.py:43
  240.5 45.1 %collective-permute-start.41 = (bf16[256,512]{1,0:T(8,128)(2,1)S(1)}, bf16[256,512]{1,0:T(8,128)(2,1)S(1)}, u32[]{:S(2)}, u32[]{:S(2)}) collective-permute-start(bf16[256,512]{1,0:T(8,128)(2,1)S(1)} %add_convert_fusion.5), channel_id=1, source_target_pairs={{115,96},{112,97},{113,98},{114,99},{119,100},{116,101},{117,102},... | collective-permute-start | bytes 786440 | tf_op jit(solution)/shard_map/ppermute | solution.py:43
  345.1 40.6 %collective-permute-start.58 = (bf16[256,512]{1,0:T(8,128)(2,1)S(1)}, bf16[256,512]{1,0:T(8,128)(2,1)S(1)}, u32[]{:S(2)}, u32[]{:S(2)}) collective-permute-start(bf16[256,512]{1,0:T(8,128)(2,1)S(1)} %add_convert_fusion.3), channel_id=1, source_target_pairs={{112,96},{113,97},{114,98},{115,99},{116,100},{117,101},{118,102},... | collective-permute-start | bytes 786440 | tf_op jit(solution)/shard_map/ppermute | solution.py:43
  346.4 43.4 %collective-permute-start.59 = (bf16[256,512]{1,0:T(8,128)(2,1)S(1)}, bf16[256,512]{1,0:T(8,128)(2,1)S(1)}, u32[]{:S(2)}, u32[]{:S(2)}) collective-permute-start(bf16[256,512]{1,0:T(8,128)(2,1)S(1)} %add_convert_fusion.3), channel_id=1, source_target_pairs={{113,96},{114,97},{115,98},{112,99},{117,100},{118,101},{119,102},... | collective-permute-start | bytes 786440 | tf_op jit(solution)/shard_map/ppermute | solution.py:43
  347.7 44.1 %collective-permute-start.60 = (bf16[256,512]{1,0:T(8,128)(2,1)S(1)}, bf16[256,512]{1,0:T(8,128)(2,1)S(1)}, u32[]{:S(2)}, u32[]{:S(2)}) collective-permute-start(bf16[256,512]{1,0:T(8,128)(2,1)S(1)} %add_convert_fusion.3), channel_id=1, source_target_pairs={{114,96},{115,97},{112,98},{113,99},{118,100},{119,101},{116,102},... | collective-permute-start | bytes 786440 | tf_op jit(solution)/shard_map/ppermute | solution.py:43
  349.0 45.6 %collective-permute-start.61 = (bf16[256,512]{1,0:T(8,128)(2,1)S(1)}, bf16[256,512]{1,0:T(8,128)(2,1)S(1)}, u32[]{:S(2)}, u32[]{:S(2)}) collective-permute-start(bf16[256,512]{1,0:T(8,128)(2,1)S(1)} %add_convert_fusion.3), channel_id=1, source_target_pairs={{115,96},{112,97},{113,98},{114,99},{119,100},{116,101},{117,102},... | collective-permute-start | bytes 786440 | tf_op jit(solution)/shard_map/ppermute | solution.py:43
  454.0 42.0 %collective-permute-start.78 = (bf16[256,512]{1,0:T(8,128)(2,1)S(1)}, bf16[256,512]{1,0:T(8,128)(2,1)S(1)}, u32[]{:S(2)}, u32[]{:S(2)}) collective-permute-start(bf16[256,512]{1,0:T(8,128)(2,1)S(1)} %add_convert_fusion.1), channel_id=1, source_target_pairs={{112,96},{113,97},{114,98},{115,99},{116,100},{117,101},{118,102},... | collective-permute-start | bytes 786440 | tf_op jit(solution)/shard_map/ppermute | solution.py:43
  455.3 44.9 %collective-permute-start.79 = (bf16[256,512]{1,0:T(8,128)(2,1)S(1)}, bf16[256,512]{1,0:T(8,128)(2,1)S(1)}, u32[]{:S(2)}, u32[]{:S(2)}) collective-permute-start(bf16[256,512]{1,0:T(8,128)(2,1)S(1)} %add_convert_fusion.1), channel_id=1, source_target_pairs={{113,96},{114,97},{115,98},{112,99},{117,100},{118,101},{119,102},... | collective-permute-start | bytes 786440 | tf_op jit(solution)/shard_map/ppermute | solution.py:43
  456.6 45.7 %collective-permute-start.80 = (bf16[256,512]{1,0:T(8,128)(2,1)S(1)}, bf16[256,512]{1,0:T(8,128)(2,1)S(1)}, u32[]{:S(2)}, u32[]{:S(2)}) collective-permute-start(bf16[256,512]{1,0:T(8,128)(2,1)S(1)} %add_convert_fusion.1), channel_id=1, source_target_pairs={{114,96},{115,97},{112,98},{113,99},{118,100},{119,101},{116,102},... | collective-permute-start | bytes 786440 | tf_op jit(solution)/shard_map/ppermute | solution.py:43
  457.9 47.1 %collective-permute-start.81 = (bf16[256,512]{1,0:T(8,128)(2,1)S(1)}, bf16[256,512]{1,0:T(8,128)(2,1)S(1)}, u32[]{:S(2)}, u32[]{:S(2)}) collective-permute-start(bf16[256,512]{1,0:T(8,128)(2,1)S(1)} %add_convert_fusion.1), channel_id=1, source_target_pairs={{115,96},{112,97},{113,98},{114,99},{119,100},{116,101},{117,102},... | collective-permute-start | bytes 786440 | tf_op jit(solution)/shard_map/ppermute | solution.py:43
  (143 other events, 939.2 us)
Sparse Core Ops, SparseCore 0:
  14.1 113.3 all-gather.1

commit v4 on v1

v4 whole, which is shorter than its diff:
```python
import jax
import jax.numpy as jnp
from jax import lax
from jax.experimental import pallas as pl
from jax.experimental.pallas import tpu as pltpu
from jax.sharding import PartitionSpec as P

BF = jnp.bfloat16
F32 = jnp.float32
SIDE = 4


def silu_slope(values):
    sigmoid = jax.nn.sigmoid(values)
    return sigmoid * (1.0 + values * (1.0 - sigmoid))


def slot_numbers(owner_row):
    blocks = owner_row.shape[0]
    earlier = jnp.arange(blocks)[None, :] < jnp.arange(blocks)[:, None]
    shared = owner_row[None, :] == owner_row[:, None]
    return jnp.sum(jnp.logical_and(earlier, shared).astype(jnp.int32), axis=1)


def permute_grid(block, source):
    route = []
    for row in range(SIDE):
        for col in range(SIDE):
            from_row, from_col = source(row, col)
            route.append((from_row * SIDE + from_col, row * SIDE + col))
    return lax.ppermute(block, "kfac", route)


def from_col(block, distance):
    return permute_grid(block, lambda row, col: (row, (col + distance) % SIDE))


def swap_cores(block):
    sections = lax.axis_size("section")
    return lax.ppermute(block, "section", [(i, i ^ 1) for i in range(sections)])


def pass_down(block):
    sections = lax.axis_size("section")
    return lax.ppermute(block, "section", [(i, i - 2) for i in range(2, sections)])


def sum_rows(block):
    near = permute_grid(block, lambda row, col: (row ^ 1, col))
    half = (block.astype(F32) + near.astype(F32)).astype(BF)
    far = permute_grid(half, lambda row, col: (SIDE - 1 - row, col))
    return half.astype(F32) + far.astype(F32)


def exchange(pieces, groups):
    return lax.all_to_all(pieces, "kfac", 0, 0, axis_index_groups=groups)


ROW_GROUPS = [[row * SIDE + col for col in range(SIDE)] for row in range(SIDE)]
COL_GROUPS = [[row * SIDE + col for row in range(SIDE)] for col in range(SIDE)]


def dot_nt(left, right):
    return lax.dot_general(left, right, (((1,), (1,)), ((), ())), preferred_element_type=F32)


def dot_nn(left, right):
    return lax.dot_general(left, right, (((1,), (0,)), ((), ())), preferred_element_type=F32)


def whole(count):
    return [pl.BlockSpec(memory_space=pltpu.VMEM)] * count


def cut_kernel(source_ref, out_ref):
    width = out_ref.shape[2]
    for j in range(out_ref.shape[0]):
        out_ref[j] = source_ref[:, j * width : (j + 1) * width]


def cut_columns(source, count):
    height, width = source.shape
    return pl.pallas_call(
        cut_kernel,
        in_specs=whole(1),
        out_specs=pl.BlockSpec(memory_space=pltpu.VMEM),
        out_shape=jax.ShapeDtypeStruct((count, height, width // count), source.dtype),
        cost_estimate=pl.CostEstimate(
            flops=0, bytes_accessed=4 * height * width, transcendentals=0
        ),
    )(source)


def back_kernel(shard_ref, *refs):
    out_ref = refs[-1]
    shard = shard_ref[...]
    start = 0
    for weight_ref in refs[:-1]:
        size = weight_ref.shape[0]
        out_ref[:, start : start + size] = dot_nt(shard, weight_ref[...]).astype(out_ref.dtype)
        start += size


def back_product(shard, weights):
    tokens, depth = shard.shape
    block = sum(w.shape[0] for w in weights)
    return pl.pallas_call(
        back_kernel,
        in_specs=whole(1 + len(weights)),
        out_specs=pl.BlockSpec(memory_space=pltpu.VMEM),
        out_shape=jax.ShapeDtypeStruct((tokens, block), BF),
        cost_estimate=pl.CostEstimate(
            flops=2 * tokens * depth * block,
            bytes_accessed=2 * depth * (tokens + block) + 2 * tokens * block,
            transcendentals=0,
        ),
    )(shard, *weights)


def proj_kernel(slope_ref, own_ref, ahead_ref, top_ref, bottom_ref, behind_ref, sent_ref, sum_ref):
    size = own_ref.shape[1]
    half = top_ref.shape[0]
    first = slope_ref[:, :size]
    second = slope_ref[:, size : 2 * size]
    third = slope_ref[:, 2 * size : 3 * size]
    fourth = slope_ref[:, 3 * size :]
    for start, far_ref in ((0, top_ref), (half, bottom_ref)):
        here = slice(start, start + half)
        total = dot_nt(first, own_ref[here, :]) + dot_nt(second, ahead_ref[here, :])
        total = total + dot_nt(third, far_ref[...]) + dot_nt(fourth, behind_ref[here, :])
        sum_ref[:, here] = total
        sent_ref[:, here] = total.astype(sent_ref.dtype)


def proj_product(slope, weights):
    tokens, block = slope.shape
    width = weights[0].shape[0]
    return pl.pallas_call(
        proj_kernel,
        in_specs=whole(1 + len(weights)),
        out_specs=whole(2),
        out_shape=[
            jax.ShapeDtypeStruct((tokens, width), BF),
            jax.ShapeDtypeStruct((tokens, width), F32),
        ],
        cost_estimate=pl.CostEstimate(
            flops=2 * tokens * width * block,
            bytes_accessed=2 * block * (tokens + width) + 6 * tokens * width,
            transcendentals=0,
        ),
    )(slope, *weights)


def after(value, *others):
    return lax.optimization_barrier((value,) + others)[0]


def spin_first(block):
    return from_col(block, 1), from_col(block, SIDE - 1)


def spin_second(ahead, behind):
    half = ahead.shape[0] // 2
    return from_col(ahead[:half], 1), from_col(behind[half:], SIDE - 1)


def left_kernel(block_ref, factor_ref, x_ref, out_ref):
    out_ref[...] = dot_nt(factor_ref[...], x_ref[...]).astype(out_ref.dtype)


def left_product(block_here, factor, x):
    size = factor.shape[0]
    tokens = x.shape[0]
    return pl.pallas_call(
        left_kernel,
        grid_spec=pltpu.PrefetchScalarGridSpec(
            num_scalar_prefetch=1,
            grid=(1,),
            in_specs=[
                pl.BlockSpec((size, size), lambda i, block: (0, 0)),
                pl.BlockSpec((tokens, size), lambda i, block: (0, block[0])),
            ],
            out_specs=pl.BlockSpec((size, tokens), lambda i, block: (0, 0)),
        ),
        out_shape=jax.ShapeDtypeStruct((size, tokens), BF),
        cost_estimate=pl.CostEstimate(
            flops=2 * size * size * tokens,
            bytes_accessed=2 * size * (size + 2 * tokens),
            transcendentals=0,
        ),
    )(block_here, factor, x)


def spread_kernel(slots_ref, left_ref, right_ref, out_ref):
    out_ref[...] = dot_nn(left_ref[...], right_ref[...]).astype(out_ref.dtype)


def spread(slots, left, right, height):
    depth = left.shape[1]
    width = right.shape[1]
    block_count = slots.shape[0]
    return pl.pallas_call(
        spread_kernel,
        grid_spec=pltpu.PrefetchScalarGridSpec(
            num_scalar_prefetch=1,
            grid=(block_count,),
            in_specs=[
                pl.BlockSpec((height, depth), lambda b, slots: (slots[b], 0)),
                pl.BlockSpec((depth, width), lambda b, slots: (0, 0)),
            ],
            out_specs=pl.BlockSpec((height, width), lambda b, slots: (b, 0)),
        ),
        out_shape=jax.ShapeDtypeStruct((block_count * height, width), BF),
        cost_estimate=pl.CostEstimate(
            flops=2 * block_count * height * depth * width,
            bytes_accessed=2 * block_count * height * (depth + width),
            transcendentals=0,
        ),
    )(slots, left, right)


def on_device(
    top_cotangent, inputs, proj_weight, return_weight, owners, input_inverses, output_inverses
):
    section_count = lax.axis_size("section")
    section_here = lax.axis_index("section")
    kfac_here = lax.axis_index("kfac")
    row, col = kfac_here // SIDE, kfac_here % SIDE
    core, plane = section_here % 2, section_here // 2
    odd_here = core == 1
    micro, per_micro, shard_width = top_cotangent.shape
    tokens = micro * per_micro
    group_tokens = tokens // SIDE
    x = inputs[0].reshape(tokens, -1)
    weight = proj_weight[0]
    width, stripe = weight.shape
    quarter = width // SIDE
    pair = SIDE // 2
    block_width = input_inverses.shape[2]
    block_count = width // block_width

    back_pieces = exchange(cut_columns(return_weight[0], SIDE), COL_GROUPS)
    proj_pieces = exchange(weight.reshape(SIDE, quarter, stripe), COL_GROUPS)

    def split(pieces):
        kept = lax.dynamic_slice_in_dim(pieces, pair * core, pair, 0)
        sent = lax.dynamic_slice_in_dim(pieces, pair * (1 - core), pair, 0)
        return kept, swap_cores(sent)

    def odd_even(kept, received):
        return jnp.where(odd_here, kept, received), jnp.where(odd_here, received, kept)

    def side_by_side(pieces):
        return jnp.concatenate([pieces[i] for i in range(pair)], axis=1)

    back_odd, back_even = odd_even(*[p.reshape(-1, quarter) for p in split(back_pieces)])
    proj_odd, proj_even = odd_even(*[side_by_side(p) for p in split(proj_pieces)])
    gathered = []
    ready = ()
    for block in (back_odd, proj_odd, back_even, proj_even):
        block = after(block, *ready)
        ready = spin_first(block)
        gathered.append([block, ready[0], *spin_second(*ready), ready[1]])
    chain_weights = ((gathered[0], gathered[1]), (gathered[2], gathered[3]))

    top = exchange(top_cotangent.reshape(SIDE, group_tokens, shard_width), ROW_GROUPS)
    shard = jnp.concatenate([top[i] for i in range(SIDE)], axis=1)

    slopes = silu_slope(dot_nn(x, weight)).reshape(1, SIDE, group_tokens, stripe)
    slopes = jnp.broadcast_to(slopes, (SIDE, SIDE, group_tokens, stripe))
    slopes = lax.all_to_all(slopes.reshape(SIDE * SIDE, group_tokens, stripe), "kfac", 0, 0)
    slopes = slopes.reshape(SIDE, SIDE, group_tokens, stripe)

    def in_ring_order(by_col):
        twice = jnp.concatenate([by_col, by_col], axis=1)
        return lax.dynamic_slice_in_dim(twice, col, SIDE, 1)

    factors = [
        jnp.transpose(in_ring_order(part), (2, 1, 0, 3)).reshape(group_tokens, -1)
        for part in odd_even(*split(slopes))
    ]

    group_here = row // pair
    out_rows = lax.dynamic_slice(
        output_inverses[0],
        (group_here, 0, row % pair * SIDE * stripe),
        (1, block_width, SIDE * stripe),
    ).reshape(pair, SIDE, stripe, SIDE * stripe)
    out_rows = jnp.swapaxes(in_ring_order(out_rows), 0, 1).reshape(block_width, SIDE * stripe)

    targets = owners[0] + slot_numbers(owners[0])
    mine = targets == kfac_here
    block_here = jnp.sum(jnp.where(mine, jnp.arange(block_count, dtype=jnp.int32), 0))
    left_here = left_product(block_here[None], input_inverses[0, 0], x)

    saved = None
    for visit in range(section_count // 2):
        new = []
        for factor, (back_weights, proj_weights) in zip(factors, chain_weights):
            back = sum_rows(back_product(shard, back_weights))
            slope = (back * factor).astype(BF)
            sent, own = proj_product(slope, proj_weights)
            summed = shard.astype(F32) + own + swap_cores(sent).astype(F32)
            shard = summed.astype(BF)
            new += [slope, shard]
        active = plane == section_count // 2 - 1 - visit
        saved = new if saved is None else [jnp.where(active, n, o) for n, o in zip(new, saved)]
        if visit == 0:
            left_all = lax.all_gather(after(left_here, shard), "kfac", axis=0, tiled=True)
        if visit < section_count // 2 - 1:
            shard = pass_down(shard)

    slope_odd, shard_odd, slope_even, shard_even = saved
    slope_mine = jnp.where(odd_here, slope_odd, slope_even)
    slope_other = swap_cores(jnp.where(odd_here, slope_even, slope_odd))
    slope_group = jnp.where(core == group_here, slope_mine, slope_other)
    right = dot_nn(slope_group, out_rows).astype(BF).reshape(group_tokens, SIDE, stripe)
    output = jnp.where(odd_here, shard_odd, shard_even).reshape(group_tokens, SIDE, shard_width)
    both = jnp.swapaxes(jnp.concatenate([output, right], axis=2), 0, 1)
    both = exchange(both, ROW_GROUPS).reshape(tokens, shard_width + stripe)
    outputs, right = both[:, :shard_width], both[:, shard_width:]
    result = spread(targets, left_all, right, block_width)
    return outputs.reshape(1, micro, per_micro, shard_width), result[None]


def solution(mesh):
    return jax.shard_map(
        on_device,
        mesh=mesh,
        in_specs=(
            P(None, None, "kfac"),
            P("section", None, None, None),
            P("section", None, "kfac"),
            P("section", "kfac", None),
            P("section", None),
            P("section", "kfac", None, None),
            P("section", None, None, None),
        ),
        out_specs=(P("section", None, None, "kfac"), P("section", None, "kfac")),
        check_vma=False,
    )
```

time: 850 us -> 475 us (0.56)
  starting transfers between devices: 581 us -> 54.3 us
  waiting for transfers between devices: 98.9 us -> 218 us
  matrix products: 101 us -> 3.79 us
  Pallas kernels: 4.87 us -> 85.3 us
  blocking collectives: 0 us -> 41.1 us
  other arithmetic: 7.23 us -> 30.7 us
  local copies, waits for them, and re-layouts: 34.6 us -> 25.7 us
    ppermute x91 -> x47, starting transfers between devices: 581 us -> 41.2 us  [the longest x32 36.4 us: permute_grid(): return lax.ppermute(block, 'kfac', route)]
    dot_general x65 -> x0, matrix products: 94.8 us -> none  [dot_nt(): lax.dot_general(left, right, (((1,), (1,)), ((), ())), preferred_element_...]
    ppermute x91 -> x47, waiting for transfers between devices: 98.9 us -> 178 us  [the longest x32 142 us: permute_grid(): return lax.ppermute(block, 'kfac', route)]
    pallas_call x0 -> x18, Pallas kernels: none -> 77.5 us  [the longest x8 36.1 us: proj_product(): pl.pallas_call(proj_kernel, in_specs=whole(1 + len(weights)), out_specs=w...]
    all_to_all x0 -> x2, blocking collectives: none -> 41.1 us  [exchange(): return lax.all_to_all(pieces, 'kfac', 0, 0, axis_index_groups=groups)]
    all_to_all x0 -> x3, waiting for transfers between devices: none -> 39.2 us  [the longest x2 38.3 us: exchange(): return lax.all_to_all(pieces, 'kfac', 0, 0, axis_index_groups=groups)]
    all_to_all x0 -> x3, starting transfers between devices: none -> 13.1 us  [the longest x2 7.86 us: exchange(): return lax.all_to_all(pieces, 'kfac', 0, 0, axis_index_groups=groups)]
    convert_element_type x6 -> x15, other arithmetic: 2.95 us -> 15.9 us  [the longest x7 8.61 us: on_device(): shard = summed.astype(BF)]
  transfers between devices with their start and end apart: 92 -> 51, of which waited for: 7 -> 38; matrix products, arithmetic and copies ran while one was open for 12% -> 12% of each run, Pallas kernels for 0% -> 15%
where the time goes in v4:
time: 475 us; the launch traced here: 473 us
  waiting for transfers between devices  218 us (46%)
  Pallas kernels  85.3 us (18%)
  starting transfers between devices  54.3 us (11%)
  blocking collectives  41.1 us (9%)
  other arithmetic  30.7 us (6%)
  local copies, waits for them, and re-layouts  25.7 us (5%)
  between operations  14.7 us (3%)
    ppermute x32, waiting for transfers between devices, permute_grid(): return lax.ppermute(block, 'kfac', route)  142 us
    all_to_all x2, blocking collectives, exchange(): return lax.all_to_all(pieces, 'kfac', 0, 0, axis_index_groups=groups)  41.1 us
    all_to_all x2, waiting for transfers between devices, exchange(): return lax.all_to_all(pieces, 'kfac', 0, 0, axis_index_groups=groups)  38.3 us
    ppermute x32, starting transfers between devices, permute_grid(): return lax.ppermute(block, 'kfac', route)  36.4 us
    pallas_call x8, Pallas kernels, proj_product(): pl.pallas_call(proj_kernel, in_specs=whole(1 + len(weights)), out_specs=w...  36.1 us
    pallas_call x8, Pallas kernels, back_product(): pl.pallas_call(back_kernel, in_specs=whole(1 + len(weights)), out_specs=p...  34.5 us
    ppermute x3, waiting for transfers between devices, pass_down(): lax.ppermute(block, 'section', [(i, i - 2) for i in range(2, sections)])  27.4 us
    slice x8, local copies, waits for them, and re-layouts, spin_second(): return (from_col(ahead[:half], 1), from_col(behind[half:], SIDE - 1))  10.6 us
  transfers between devices with their start and end apart: 51, of which 38 were waited for; matrix products, arithmetic and copies ran while one was open for 12% of the time, Pallas kernels for 15%

profile of v4, /device:TPU:0, one launch (start us, length us, event | category | flops | bytes accessed | tf_op | source)
XLA Modules:
  0.0 473.3 jit_solution(16979507387970613687)
XLA Ops:
  10.2 30.9 %all_to_all.25 = bf16[4,128,2048]{2,1,0:T(8,128)(2,1)S(1)} all-to-all(bf16[4,128,2048]{2,1,0:T(8,128)(2,1)} %shard_map.86), channel_id=1, replica_groups={{0,4,8,12},{1,5,9,13},{2,6,10,14},{3,7,11,15},{16,20,24,28},{17,21,25,2..., dimensions={0} | all-to-all | bytes 4194304 | tf_op jit(solution)/shard_map/all_to_all | solution.py:56
  45.8 25.2 %all-to-all-done.3 = bf16[4,2048,128]{2,1,0:T(8,128)(2,1)} async-done(((bf16[4,2048,128]{2,1,0:T(8,128)(2,1)}), bf16[4,2048,128]{2,1,0:T(8,128)(2,1)}, u32[]{:S(2)}, u32[]{:S(2)}) %all-to-all-start.3) | async-done | bytes 2097184 | tf_op jit(solution)/shard_map/all_to_all | solution.py:56
  81.6 19.0 %collective-permute-done.1.refs_1_ = bf16[256,2048]{1,0:T(8,128)(2,1)} collective-permute-done((bf16[256,2048]{1,0:T(8,128)(2,1)S(1)}, bf16[256,2048]{1,0:T(8,128)(2,1)}, u32[]{:S(2)}, u32[]{:S(2)}) %collective-permute-start.1) | collective-permute-done | bytes 1048608 | tf_op jit(solution)/shard_map/ppermute | solution.py:31
  121.4 13.0 %all-to-all-done = bf16[4,64,512]{2,1,0:T(8,128)(2,1)S(1)} async-done(((bf16[4,64,512]{2,1,0:T(8,128)(2,1)}), bf16[4,64,512]{2,1,0:T(8,128)(2,1)S(1)}, u32[]{:S(2)}, u32[]{:S(2)}) %all-to-all-start) | async-done | bytes 262176 | tf_op jit(solution)/shard_map/all_to_all | solution.py:56
  135.4 5.3 %all-to-all-start.2 = ((f32[16,64,128]{2,1,0:T(8,128)}), f32[16,64,128]{2,1,0:T(8,128)}, u32[]{:S(2)}, u32[]{:S(2)}) async-start(f32[16,64,128]{2,1,0:T(8,128)} %bitcast.75), calls=%async_computation.2 | async-start | bytes 1048576 | tf_op jit(solution)/shard_map/all_to_all | solution.py:271
  178.8 5.9 %collective-permute-done.10.top_ref = bf16[1024,256]{1,0:T(8,128)(2,1)} collective-permute-done((bf16[1024,256]{1,0:T(8,128)(2,1)}, bf16[1024,256]{1,0:T(8,128)(2,1)}, u32[]{:S(2)}, u32[]{:S(2)}) %collective-permute-start.10) | collective-permute-done | bytes 524320 | tf_op jit(solution)/shard_map/ppermute | solution.py:31
  196.3 20.1 %collective-permute-done.15.refs_2_ = bf16[128,2048]{1,0:T(8,128)(2,1)} collective-permute-done((bf16[128,2048]{1,0:T(8,128)(2,1)S(1)}, bf16[128,2048]{1,0:T(8,128)(2,1)}, u32[]{:S(2)}, u32[]{:S(2)}) %collective-permute-start.15) | collective-permute-done | bytes 524320 | tf_op jit(solution)/shard_map/ppermute | solution.py:31
  228.7 4.7 collective-permute-done.19
  251.8 9.5 %collective-permute-done.25.shard_ref = bf16[64,2048]{1,0:T(8,128)(2,1)S(1)} collective-permute-done((bf16[64,2048]{1,0:T(8,128)(2,1)S(1)}, bf16[64,2048]{1,0:T(8,128)(2,1)S(1)}, u32[]{:S(2)}, u32[]{:S(2)}) %collective-permute-start.25) | collective-permute-done | bytes 262176 | tf_op jit(solution)/shard_map/ppermute | solution.py:45
  267.8 7.3 %collective-permute-done.26 = bf16[64,1024]{1,0:T(8,128)(2,1)S(1)} collective-permute-done((bf16[64,1024]{1,0:T(8,128)(2,1)}, bf16[64,1024]{1,0:T(8,128)(2,1)S(1)}, u32[]{:S(2)}, u32[]{:S(2)}) %collective-permute-start.26) | collective-permute-done | bytes 131104 | tf_op jit(solution)/shard_map/ppermute | solution.py:31
  277.0 5.3 %collective-permute-done.27 = bf16[64,1024]{1,0:T(8,128)(2,1)S(1)} collective-permute-done((bf16[64,1024]{1,0:T(8,128)(2,1)S(1)}, bf16[64,1024]{1,0:T(8,128)(2,1)S(1)}, u32[]{:S(2)}, u32[]{:S(2)}) %collective-permute-start.27) | collective-permute-done | bytes 131104 | tf_op jit(solution)/shard_map/ppermute | solution.py:31
  295.4 9.1 %collective-permute-done.29 = bf16[64,1024]{1,0:T(8,128)(2,1)S(1)} collective-permute-done((bf16[64,1024]{1,0:T(8,128)(2,1)}, bf16[64,1024]{1,0:T(8,128)(2,1)S(1)}, u32[]{:S(2)}, u32[]{:S(2)}) %collective-permute-start.29) | collective-permute-done | bytes 131104 | tf_op jit(solution)/shard_map/ppermute | solution.py:31
  306.4 9.0 %collective-permute-done.30 = bf16[64,1024]{1,0:T(8,128)(2,1)S(1)} collective-permute-done((bf16[64,1024]{1,0:T(8,128)(2,1)S(1)}, bf16[64,1024]{1,0:T(8,128)(2,1)S(1)}, u32[]{:S(2)}, u32[]{:S(2)}) %collective-permute-start.30) | collective-permute-done | bytes 131104 | tf_op jit(solution)/shard_map/ppermute | solution.py:31
  324.8 9.0 %collective-permute-done.32.shard_ref = bf16[64,2048]{1,0:T(8,128)(2,1)S(1)} collective-permute-done((bf16[64,2048]{1,0:T(8,128)(2,1)S(1)}, bf16[64,2048]{1,0:T(8,128)(2,1)S(1)}, u32[]{:S(2)}, u32[]{:S(2)}) %collective-permute-start.32) | collective-permute-done | bytes 262176 | tf_op jit(solution)/shard_map/ppermute | solution.py:45
  338.8 5.2 %collective-permute-done.33 = bf16[64,1024]{1,0:T(8,128)(2,1)S(1)} collective-permute-done((bf16[64,1024]{1,0:T(8,128)(2,1)}, bf16[64,1024]{1,0:T(8,128)(2,1)S(1)}, u32[]{:S(2)}, u32[]{:S(2)}) %collective-permute-start.33) | collective-permute-done | bytes 131104 | tf_op jit(solution)/shard_map/ppermute | solution.py:31
  346.2 5.2 %collective-permute-done.34 = bf16[64,1024]{1,0:T(8,128)(2,1)S(1)} collective-permute-done((bf16[64,1024]{1,0:T(8,128)(2,1)S(1)}, bf16[64,1024]{1,0:T(8,128)(2,1)S(1)}, u32[]{:S(2)}, u32[]{:S(2)}) %collective-permute-start.34) | collective-permute-done | bytes 131104 | tf_op jit(solution)/shard_map/ppermute | solution.py:31
  364.5 5.7 %collective-permute-done.36 = bf16[64,1024]{1,0:T(8,128)(2,1)S(1)} collective-permute-done((bf16[64,1024]{1,0:T(8,128)(2,1)}, bf16[64,1024]{1,0:T(8,128)(2,1)S(1)}, u32[]{:S(2)}, u32[]{:S(2)}) %collective-permute-start.36) | collective-permute-done | bytes 131104 | tf_op jit(solution)/shard_map/ppermute | solution.py:31
  372.3 5.2 %collective-permute-done.37 = bf16[64,1024]{1,0:T(8,128)(2,1)S(1)} collective-permute-done((bf16[64,1024]{1,0:T(8,128)(2,1)S(1)}, bf16[64,1024]{1,0:T(8,128)(2,1)S(1)}, u32[]{:S(2)}, u32[]{:S(2)}) %collective-permute-start.37) | collective-permute-done | bytes 131104 | tf_op jit(solution)/shard_map/ppermute | solution.py:31
  386.9 9.0 %collective-permute-done.39.shard_ref = bf16[64,2048]{1,0:T(8,128)(2,1)S(1)} collective-permute-done((bf16[64,2048]{1,0:T(8,128)(2,1)S(1)}, bf16[64,2048]{1,0:T(8,128)(2,1)S(1)}, u32[]{:S(2)}, u32[]{:S(2)}) %collective-permute-start.39) | collective-permute-done | bytes 262176 | tf_op jit(solution)/shard_map/ppermute | solution.py:45
  400.8 5.2 %collective-permute-done.40 = bf16[64,1024]{1,0:T(8,128)(2,1)S(1)} collective-permute-done((bf16[64,1024]{1,0:T(8,128)(2,1)}, bf16[64,1024]{1,0:T(8,128)(2,1)S(1)}, u32[]{:S(2)}, u32[]{:S(2)}) %collective-permute-start.40) | collective-permute-done | bytes 131104 | tf_op jit(solution)/shard_map/ppermute | solution.py:31
  408.1 5.2 %collective-permute-done.41 = bf16[64,1024]{1,0:T(8,128)(2,1)S(1)} collective-permute-done((bf16[64,1024]{1,0:T(8,128)(2,1)S(1)}, bf16[64,1024]{1,0:T(8,128)(2,1)S(1)}, u32[]{:S(2)}, u32[]{:S(2)}) %collective-permute-start.41) | collective-permute-done | bytes 131104 | tf_op jit(solution)/shard_map/ppermute | solution.py:31
  426.5 5.7 %collective-permute-done.43 = bf16[64,1024]{1,0:T(8,128)(2,1)S(1)} collective-permute-done((bf16[64,1024]{1,0:T(8,128)(2,1)}, bf16[64,1024]{1,0:T(8,128)(2,1)S(1)}, u32[]{:S(2)}, u32[]{:S(2)}) %collective-permute-start.43) | collective-permute-done | bytes 131104 | tf_op jit(solution)/shard_map/ppermute | solution.py:31
  447.1 10.2 %all_to_all.26 = bf16[4,64,640]{2,1,0:T(8,128)(2,1)S(1)} all-to-all(bf16[4,64,640]{2,1,0:T(8,128)(2,1)S(1)} %maximum_bitcast_fusion), channel_id=1, replica_groups={{0,1,2,3},{4,5,6,7},{8,9,10,11},{12,13,14,15},{16,17,18,19},{20,21,22,2..., dimensions={0} | all-to-all | bytes 655360 | tf_op jit(solution)/shard_map/all_to_all | solution.py:56
  458.7 7.8 %shard_map.104 = bf16[8192,128]{1,0:T(8,128)(2,1)} custom-call(s32[8]{0:T(128)} %get-tuple-element.43.slots_ref, bf16[16384,256]{1,0:T(8,128)(2,1)} %all-gather.2.cloned.1.call-done.left_ref, bf16[256,128]{1,0:T(8,128)(2,1)} %slice.87.right_ref), custom_call_target="tpu_custom_call" | custom-call | flops 536870912 | bytes 6291456 | tf_op jit(solution)/shard_map/pallas_call | solution.py:202
  (244 shorter events, 221.2 us)
Async XLA Ops:
  41.1 29.9 %all-to-all-start.3 = ((bf16[4,2048,128]{2,1,0:T(8,128)(2,1)}), bf16[4,2048,128]{2,1,0:T(8,128)(2,1)}, u32[]{:S(2)}, u32[]{:S(2)}) async-start(bf16[4,2048,128]{2,1,0:T(8,128)(2,1)} %bitcast.77), calls=%async_computation.3 | async-start | bytes 4194304 | tf_op jit(solution)/shard_map/all_to_all | solution.py:56
  45.7 27.6 %collective-permute-start = (bf16[2,128,2048]{2,1,0:T(8,128)(2,1)S(1)}, bf16[2,128,2048]{2,1,0:T(8,128)(2,1)S(1)}, u32[]{:S(2)}, u32[]{:S(2)}) collective-permute-start(bf16[2,128,2048]{2,1,0:T(8,128)(2,1)S(1)} %constant_dynamic-slice_fusion.3), channel_id=1, source_target_pairs={{0,16},{16,0},{32,48},{48,32},{64,80},{80,64},{96,112},{112,96},{1... | collective-permute-start | bytes 3145736 | tf_op jit(solution)/shard_map/ppermute | solution.py:40
  74.7 25.9 %collective-permute-start.1 = (bf16[256,2048]{1,0:T(8,128)(2,1)S(1)}, bf16[256,2048]{1,0:T(8,128)(2,1)}, u32[]{:S(2)}, u32[]{:S(2)}) collective-permute-start(bf16[256,2048]{1,0:T(8,128)(2,1)S(1)} %bitcast.65), channel_id=1, source_target_pairs={{1,0},{2,1},{3,2},{0,3},{5,4},{6,5},{7,6},{4,7},{9,8},{10,9},{11,1... | collective-permute-start | bytes 3145736 | tf_op jit(solution)/shard_map/ppermute | solution.py:31
  77.6 26.6 %collective-permute-start.3 = (bf16[256,2048]{1,0:T(8,128)(2,1)S(1)}, bf16[256,2048]{1,0:T(8,128)(2,1)}, u32[]{:S(2)}, u32[]{:S(2)}) collective-permute-start(bf16[256,2048]{1,0:T(8,128)(2,1)S(1)} %bitcast.66), channel_id=1, source_target_pairs={{3,0},{0,1},{1,2},{2,3},{7,4},{4,5},{5,6},{6,7},{11,8},{8,9},{9,10... | collective-permute-start | bytes 3145736 | tf_op jit(solution)/shard_map/ppermute | solution.py:31
  104.2 36.5 %collective-permute-start.11 = (bf16[2048,256]{1,0:T(8,128)(2,1)}, bf16[2048,256]{1,0:T(8,128)(2,1)S(1)}, u32[]{:S(2)}, u32[]{:S(2)}) collective-permute-start(bf16[2048,256]{1,0:T(8,128)(2,1)} %get-tuple-element.22.own_ref), channel_id=1, source_target_pairs={{3,0},{0,1},{1,2},{2,3},{7,4},{4,5},{5,6},{6,7},{11,8},{8,9},{9,10... | collective-permute-start | bytes 3145736 | tf_op jit(solution)/shard_map/ppermute | solution.py:31
  104.2 36.5 %collective-permute-start.9 = (bf16[2048,256]{1,0:T(8,128)(2,1)}, bf16[2048,256]{1,0:T(8,128)(2,1)}, u32[]{:S(2)}, u32[]{:S(2)}) collective-permute-start(bf16[2048,256]{1,0:T(8,128)(2,1)} %get-tuple-element.22.own_ref), channel_id=1, source_target_pairs={{1,0},{2,1},{3,2},{0,3},{5,4},{6,5},{7,6},{4,7},{9,8},{10,9},{11,1... | collective-permute-start | bytes 3145736 | tf_op jit(solution)/shard_map/ppermute | solution.py:31
  107.4 27.1 %all-to-all-start = ((bf16[4,64,512]{2,1,0:T(8,128)(2,1)}), bf16[4,64,512]{2,1,0:T(8,128)(2,1)S(1)}, u32[]{:S(2)}, u32[]{:S(2)}) async-start(bf16[4,64,512]{2,1,0:T(8,128)(2,1)} %bitcast.85), calls=%async_computation | async-start | bytes 524288 | tf_op jit(solution)/shard_map/all_to_all | solution.py:56
  112.9 35.0 %collective-permute-start.2 = (bf16[128,2048]{1,0:T(8,128)(2,1)}, bf16[128,2048]{1,0:T(8,128)(2,1)}, u32[]{:S(2)}, u32[]{:S(2)}) collective-permute-start(bf16[128,2048]{1,0:T(8,128)(2,1)} %slice.76), channel_id=1, source_target_pairs={{1,0},{2,1},{3,2},{0,3},{5,4},{6,5},{7,6},{4,7},{9,8},{10,9},{11,1... | collective-permute-start | bytes 1572872 | tf_op jit(solution)/shard_map/ppermute | solution.py:31
  117.9 30.4 %collective-permute-start.4 = (bf16[128,2048]{1,0:T(8,128)(2,1)}, bf16[128,2048]{1,0:T(8,128)(2,1)}, u32[]{:S(2)}, u32[]{:S(2)}) collective-permute-start(bf16[128,2048]{1,0:T(8,128)(2,1)} %slice.77), channel_id=1, source_target_pairs={{3,0},{0,1},{1,2},{2,3},{7,4},{4,5},{5,6},{6,7},{11,8},{8,9},{9,10... | collective-permute-start | bytes 1572872 | tf_op jit(solution)/shard_map/ppermute | solution.py:31
  135.4 18.3 %all-to-all-start.2 = ((f32[16,64,128]{2,1,0:T(8,128)}), f32[16,64,128]{2,1,0:T(8,128)}, u32[]{:S(2)}, u32[]{:S(2)}) async-start(f32[16,64,128]{2,1,0:T(8,128)} %bitcast.75), calls=%async_computation.2 | async-start | bytes 1048576 | tf_op jit(solution)/shard_map/all_to_all | solution.py:271
  140.6 318.0 %all-gather.2.cloned.1.call-start = ((), (), s32[]{:S(2)}) async-start(), calls=%async_computation.5 | async-start | bytes 8912896 | tf_op jit(solution)/shard_map/all_gather | solution.py:309
  140.7 32.6 %collective-permute-start.14 = (bf16[256,2048]{1,0:T(8,128)(2,1)S(1)}, bf16[256,2048]{1,0:T(8,128)(2,1)}, u32[]{:S(2)}, u32[]{:S(2)}) collective-permute-start(bf16[256,2048]{1,0:T(8,128)(2,1)S(1)} %bitcast.59), channel_id=1, source_target_pairs={{1,0},{2,1},{3,2},{0,3},{5,4},{6,5},{7,6},{4,7},{9,8},{10,9},{11,1... | collective-permute-start | bytes 3145736 | tf_op jit(solution)/shard_map/ppermute | solution.py:31
  143.9 30.0 %collective-permute-start.16 = (bf16[256,2048]{1,0:T(8,128)(2,1)S(1)}, bf16[256,2048]{1,0:T(8,128)(2,1)}, u32[]{:S(2)}, u32[]{:S(2)}) collective-permute-start(bf16[256,2048]{1,0:T(8,128)(2,1)S(1)} %bitcast.60), channel_id=1, source_target_pairs={{3,0},{0,1},{1,2},{2,3},{7,4},{4,5},{5,6},{6,7},{11,8},{8,9},{9,10... | collective-permute-start | bytes 3145736 | tf_op jit(solution)/shard_map/ppermute | solution.py:31
  155.3 11.3 %collective-permute-start.7 = (f32[2,4,64,128]{3,2,1,0:T(8,128)}, f32[2,4,64,128]{3,2,1,0:T(8,128)S(1)}, u32[]{:S(2)}, u32[]{:S(2)}) collective-permute-start(f32[2,4,64,128]{3,2,1,0:T(8,128)} %constant_dynamic-slice_fusion.2), channel_id=1, source_target_pairs={{0,16},{16,0},{32,48},{48,32},{64,80},{80,64},{96,112},{112,96},{1... | collective-permute-start | bytes 786440 | tf_op jit(solution)/shard_map/ppermute | solution.py:40
  159.5 17.7 %collective-permute-start.6 = (bf16[64,1024]{1,0:T(8,128)(2,1)}, bf16[64,1024]{1,0:T(8,128)(2,1)}, u32[]{:S(2)}, u32[]{:S(2)}) collective-permute-start(bf16[64,1024]{1,0:T(8,128)(2,1)} %add_convert_fusion.15), channel_id=1, source_target_pairs={{12,0},{13,1},{14,2},{15,3},{8,4},{9,5},{10,6},{11,7},{4,8},{5,9},... | collective-permute-start | bytes 393224 | tf_op jit(solution)/shard_map/ppermute | solution.py:31
  162.0 22.7 %collective-permute-start.10 = (bf16[1024,256]{1,0:T(8,128)(2,1)}, bf16[1024,256]{1,0:T(8,128)(2,1)}, u32[]{:S(2)}, u32[]{:S(2)}) collective-permute-start(bf16[1024,256]{1,0:T(8,128)(2,1)} %slice.80), channel_id=1, source_target_pairs={{1,0},{2,1},{3,2},{0,3},{5,4},{6,5},{7,6},{4,7},{9,8},{10,9},{11,1... | collective-permute-start | bytes 1572872 | tf_op jit(solution)/shard_map/ppermute | solution.py:31
  166.7 18.5 %collective-permute-start.12 = (bf16[1024,256]{1,0:T(8,128)(2,1)}, bf16[1024,256]{1,0:T(8,128)(2,1)}, u32[]{:S(2)}, u32[]{:S(2)}) collective-permute-start(bf16[1024,256]{1,0:T(8,128)(2,1)} %slice.81), channel_id=1, source_target_pairs={{3,0},{0,1},{1,2},{2,3},{7,4},{4,5},{5,6},{6,7},{11,8},{8,9},{9,10... | collective-permute-start | bytes 1572872 | tf_op jit(solution)/shard_map/ppermute | solution.py:31
  173.9 48.3 %collective-permute-start.20 = (bf16[2048,256]{1,0:T(8,128)(2,1)S(1)}, bf16[2048,256]{1,0:T(8,128)(2,1)S(1)}, u32[]{:S(2)}, u32[]{:S(2)}) collective-permute-start(bf16[2048,256]{1,0:T(8,128)(2,1)S(1)} %get-tuple-element.26.own_ref), channel_id=1, source_target_pairs={{1,0},{2,1},{3,2},{0,3},{5,4},{6,5},{7,6},{4,7},{9,8},{10,9},{11,1... | collective-permute-start | bytes 3145736 | tf_op jit(solution)/shard_map/ppermute | solution.py:31
  177.2 48.9 %collective-permute-start.22 = (bf16[2048,256]{1,0:T(8,128)(2,1)S(1)}, bf16[2048,256]{1,0:T(8,128)(2,1)S(1)}, u32[]{:S(2)}, u32[]{:S(2)}) collective-permute-start(bf16[2048,256]{1,0:T(8,128)(2,1)S(1)} %get-tuple-element.26.own_ref), channel_id=1, source_target_pairs={{3,0},{0,1},{1,2},{2,3},{7,4},{4,5},{5,6},{6,7},{11,8},{8,9},{9,10... | collective-permute-start | bytes 3145736 | tf_op jit(solution)/shard_map/ppermute | solution.py:31
  191.0 25.4 %collective-permute-start.15 = (bf16[128,2048]{1,0:T(8,128)(2,1)S(1)}, bf16[128,2048]{1,0:T(8,128)(2,1)}, u32[]{:S(2)}, u32[]{:S(2)}) collective-permute-start(bf16[128,2048]{1,0:T(8,128)(2,1)S(1)} %slice.82), channel_id=1, source_target_pairs={{1,0},{2,1},{3,2},{0,3},{5,4},{6,5},{7,6},{4,7},{9,8},{10,9},{11,1... | collective-permute-start | bytes 1572872 | tf_op jit(solution)/shard_map/ppermute | solution.py:31
  195.4 21.8 %collective-permute-start.17 = (bf16[128,2048]{1,0:T(8,128)(2,1)S(1)}, bf16[128,2048]{1,0:T(8,128)(2,1)}, u32[]{:S(2)}, u32[]{:S(2)}) collective-permute-start(bf16[128,2048]{1,0:T(8,128)(2,1)S(1)} %slice.83), channel_id=1, source_target_pairs={{3,0},{0,1},{1,2},{2,3},{7,4},{4,5},{5,6},{6,7},{11,8},{8,9},{9,10... | collective-permute-start | bytes 1572872 | tf_op jit(solution)/shard_map/ppermute | solution.py:31
  223.1 12.5 %collective-permute-start.21 = (bf16[1024,256]{1,0:T(8,128)(2,1)}, bf16[1024,256]{1,0:T(8,128)(2,1)}, u32[]{:S(2)}, u32[]{:S(2)}) collective-permute-start(bf16[1024,256]{1,0:T(8,128)(2,1)} %slice.84), channel_id=1, source_target_pairs={{1,0},{2,1},{3,2},{0,3},{5,4},{6,5},{7,6},{4,7},{9,8},{10,9},{11,1... | collective-permute-start | bytes 1572872 | tf_op jit(solution)/shard_map/ppermute | solution.py:31
  227.0 12.9 %collective-permute-start.23 = (bf16[1024,256]{1,0:T(8,128)(2,1)}, bf16[1024,256]{1,0:T(8,128)(2,1)S(1)}, u32[]{:S(2)}, u32[]{:S(2)}) collective-permute-start(bf16[1024,256]{1,0:T(8,128)(2,1)} %slice.85), channel_id=1, source_target_pairs={{3,0},{0,1},{1,2},{2,3},{7,4},{4,5},{5,6},{6,7},{11,8},{8,9},{9,10... | collective-permute-start | bytes 1572872 | tf_op jit(solution)/shard_map/ppermute | solution.py:31
  250.5 10.8 %collective-permute-start.25 = (bf16[64,2048]{1,0:T(8,128)(2,1)S(1)}, bf16[64,2048]{1,0:T(8,128)(2,1)S(1)}, u32[]{:S(2)}, u32[]{:S(2)}) collective-permute-start(bf16[64,2048]{1,0:T(8,128)(2,1)S(1)} %add_convert_fusion.6), channel_id=1, source_target_pairs={{32,0},{48,16},{64,32},{80,48},{96,64},{112,80},{33,1},{49,17},{65... | collective-permute-start | bytes 786440 | tf_op jit(solution)/shard_map/ppermute | solution.py:45
  (69 other events, 605.3 us)
Sparse Core Ops, SparseCore 0:
  250.6 74.7 all-gather.1
